TPU v7x, 128 devices: a whole 4x4x4 slice. The times are simulated.
128 devices in a mesh: shard: 16 (over y, z_lo, core), ctx: 2 (over z_hi), tp: 4 (over x).
Axes of the slice: x: 4, y: 4, z: 4 (z_hi: 2, z_lo: 2; z = z_hi * 2 + z_lo), core: 2. Of those that a mesh axis runs over, the one named last changes fastest.
Arguments:
- tokens: bfloat16 [32, 28, 42, 1280], P('shard', 'ctx', None, 'tp'), may hold values from -6 to 6
- valid_mask: int32 [32, 28, 42], P('shard', 'ctx'), may hold values from 0 to 1, as said below
- ln1_gain: float32 [1280], replicated, may hold values from 0.25 to 1.75
- ln1_bias: float32 [1280], replicated, may hold values from -3 to 3
- qkv_weight: bfloat16 [3, 1280, 1280], P(None, 'shard', 'tp'), may hold values from -0.15625 to 0.15625
- qkv_bias: float32 [2, 1280], P(None, 'tp'), may hold values from -3 to 3
- rel_rows: bfloat16 [27, 80], replicated, may hold values from -0.69921875 to 0.69921875
- rel_cols: bfloat16 [27, 80], replicated, may hold values from -0.69921875 to 0.69921875
- proj_weight: bfloat16 [1280, 1280], P('tp', 'shard'), may hold values from -0.625 to 0.625
- proj_bias: float32 [1280], replicated, may hold values from -3 to 3
- ln2_gain: float32 [1280], replicated, may hold values from 0.25 to 1.75
- ln2_bias: float32 [1280], replicated, may hold values from -3 to 3
- fc1_weight: bfloat16 [1280, 5120], P('shard', 'tp'), may hold values from -0.15625 to 0.15625
- fc1_bias: float32 [5120], P('tp'), may hold values from -3 to 3
- fc2_weight: bfloat16 [5120, 1280], P('tp', 'shard'), may hold values from -0.078125 to 0.078125
- fc2_bias: float32 [1280], replicated, may hold values from -3 to 3
- cotangent: bfloat16 [32, 28, 42, 1280], P('shard', 'ctx', None, 'tp'), may hold values from -6 to 6
Outputs:
- result: bfloat16 [32, 28, 42, 1280], P('shard', 'ctx', None, 'tp')
- grad_tokens: float32 [32, 28, 42, 1280], P('shard', 'ctx', None, 'tp')
- grad_ln1_gain: float32 [1280], replicated
- grad_ln1_bias: float32 [1280], replicated
- grad_qkv_weight: float32 [3, 1280, 1280], P(None, 'shard', 'tp')
- grad_qkv_bias: float32 [2, 1280], P(None, 'tp')
- grad_rel_rows: float32 [27, 80], replicated
- grad_rel_cols: float32 [27, 80], replicated
- grad_proj_weight: float32 [1280, 1280], P('tp', 'shard')
- grad_proj_bias: float32 [1280], replicated
- grad_ln2_gain: float32 [1280], replicated
- grad_ln2_bias: float32 [1280], replicated
- grad_fc1_weight: float32 [1280, 5120], P('shard', 'tp')
- grad_fc1_bias: float32 [5120], P('tp')
- grad_fc2_weight: float32 [5120, 1280], P('tp', 'shard')
- grad_fc2_bias: float32 [1280], replicated
Inputs may be any that keep to these rules, and one draw needn't show every extreme that they name: `valid_mask`: the ones of each image form a top-left rectangle of more than 14 rows and more than 28 columns.
All inputs are finite; a program needn't handle non-finite values.
Results may differ from a plain program's by a relative error of at most 0.025.
Values may be sent and summed in bfloat16 or wider, within the bound.
No kernel may reach another device: no remote copies, remote signals or barrier semaphores. Data moves between devices by JAX's collectives and lax.ppermute only.
A program may use at most 320 MiB of HBM per device.

v0:
```python
from functools import partial

import jax
import jax.numpy as jnp
from jax import lax
from jax.sharding import PartitionSpec as P

HEADS = 16
HDIM = 80
WIN = 14


epsilon = 1e-06


def rows_first(arrays, axis, dims):
    turned = [jnp.moveaxis(a, dim, 0) for a, dim in zip(arrays, dims)]
    widths = [t[0].size for t in turned]
    both = jnp.concatenate([t.reshape(-1, w) for t, w in zip(turned, widths)], axis=1)
    out = lax.all_gather(both, axis, axis=0, tiled=True)
    tiles = jnp.split(out, [sum(widths[:k]) for k in range(1, len(widths))], axis=1)
    return tuple(
        (
            jnp.moveaxis(b.reshape(-1, *t.shape[1:]), 0, dim)
            for b, t, dim in zip(tiles, turned, dims)
        )
    )


def from_everyone(array, axis):
    size = lax.axis_size(axis)
    return lax.all_to_all(
        jnp.broadcast_to(array[None], (size, *array.shape)), axis, 0, 0, tiled=True
    )


def in_order(tiles, dim):
    tiles = jnp.moveaxis(tiles, 0, dim)
    shape = tiles.shape
    return tiles.reshape(*shape[:dim], shape[dim] * shape[dim + 1], *shape[dim + 2 :])


def gathered_copies(array, axis, dim):
    tiles = from_everyone(array, axis)
    return in_order(tiles, dim)


def split_up(array, dim, size):
    before, after = (array.shape[:dim], array.shape[dim + 1 :])
    return jnp.moveaxis(array.reshape(*before, size, -1, *after), dim, 0)


def summed_on_arrival(array, axis, dim):
    tiles = split_up(array, dim, lax.axis_size(axis))
    arrived = lax.all_to_all(tiles, axis, split_axis=0, concat_axis=0, tiled=True)
    return arrived.astype(jnp.float32).sum(axis=0)


def over_copies(array, axis):
    everything = from_everyone(array, axis)
    return jnp.sum(everything, axis=0)


def in_one(arrays, axis):
    ends = [0]
    for a in arrays:
        ends.append(ends[-1] + a.size)
    so_far = over_copies(jnp.concatenate([a.ravel() for a in arrays]), axis)
    return tuple((so_far[b:e].reshape(a.shape) for a, b, e in zip(arrays, ends, ends[1:])))


def of_everyone(array, axis):
    everything = from_everyone(array, axis)
    return jnp.sum(everything.astype(jnp.float32), axis=0)


def norm_forward(values, gain_term, bias_term):
    average = jnp.mean(values, axis=-1, keepdims=True)
    centered = values - average
    inverse = lax.rsqrt(jnp.mean(centered * centered, axis=-1, keepdims=True) + epsilon)
    scaled = centered * inverse
    return (scaled * gain_term + bias_term, scaled, inverse)


def norm_backward(grad_out, scaled, inverse, gain_term):
    weighted = grad_out * gain_term
    first_mean = jnp.mean(weighted, axis=-1, keepdims=True)
    second_mean = jnp.mean(weighted * scaled, axis=-1, keepdims=True)
    return inverse * (weighted - first_mean - scaled * second_mean)


def offset_table(width_cells):
    first_pos = jnp.arange(width_cells)[:, None, None]
    second_pos = jnp.arange(width_cells)[None, :, None]
    entry_pos = jnp.arange(2 * width_cells - 1)[None, None, :]
    return (first_pos - second_pos + width_cells - 1 == entry_pos).astype(jnp.float32)


def local(
    tokens,
    valid_mask,
    ln1_gain,
    ln1_bias,
    qkv_weight,
    qkv_bias,
    rel_rows,
    rel_cols,
    proj_weight,
    proj_bias,
    ln2_gain,
    ln2_bias,
    fc1_weight,
    fc1_bias,
    fc2_weight,
    fc2_bias,
    cotangent,
):
    tp_count = lax.axis_size("tp")
    tp_index = lax.axis_index("tp")
    local_width = tokens.shape[3]
    full_width = local_width * tp_count
    heads_local = HEADS // tp_count
    inner_width = heads_local * HDIM
    grid_cols = tokens.shape[2]
    window_cols = grid_cols // WIN
    row_count = WIN * grid_cols
    cell_count = WIN * WIN
    hidden_width = fc1_bias.shape[0]
    scale_factor = HDIM ** (-0.5)
    offsets = offset_table(WIN)
    row_table = jnp.einsum("axd,dc->axc", offsets, rel_rows.astype(jnp.float32))
    col_table = jnp.einsum("axd,dc->axc", offsets, rel_cols.astype(jnp.float32))
    row_low = row_table.astype(jnp.bfloat16)
    col_low = col_table.astype(jnp.bfloat16)
    window_form = (WIN, window_cols, WIN, heads_local, HDIM)
    six_form = (window_cols, heads_local, WIN, WIN, WIN, WIN)
    local_start = tp_index * local_width
    zero_full = jnp.zeros((full_width,), jnp.float32)
    gain1_local = lax.dynamic_slice_in_dim(ln1_gain, local_start, local_width, 0)

    def score_block(query_win, key_win):
        direct = (
            jnp.einsum(
                "awbhc,xwyhc->whabxy", query_win, key_win, preferred_element_type=jnp.float32
            )
            * scale_factor
        )
        along_rows = jnp.einsum(
            "awbhc,axc->whabx", query_win, row_low, preferred_element_type=jnp.float32
        )
        along_cols = jnp.einsum(
            "awbhc,byc->whaby", query_win, col_low, preferred_element_type=jnp.float32
        )
        total_score = direct + along_rows[..., None] + along_cols[..., None, :]
        return total_score.reshape(window_cols, heads_local, cell_count, cell_count)

    def micro_step(totals, inputs):
        token_part, mask_part, cot_part = inputs
        keep_cells = mask_part.astype(jnp.float32)[..., None]
        gathered = rows_first(
            (qkv_weight, proj_weight, fc1_weight, fc2_weight), "shard", (1, 1, 0, 1)
        )
        qkv_full, proj_full, fc1_full, fc2_full = gathered
        token_grid = gathered_copies(token_part, "tp", 2).astype(jnp.float32)
        normed1, scaled1, inverse1 = norm_forward(token_grid, ln1_gain, ln1_bias)
        entering = (normed1 * keep_cells).astype(jnp.bfloat16).reshape(row_count, full_width)
        projected = jnp.einsum(
            "rd,tde->tre", entering, qkv_full, preferred_element_type=jnp.float32
        )
        queries = (projected[0] + qkv_bias[0]).astype(jnp.bfloat16).reshape(window_form)
        keys_in = projected[1].astype(jnp.bfloat16).reshape(window_form)
        values_in = (projected[2] + qkv_bias[1]).astype(jnp.bfloat16).reshape(window_form)
        scores = score_block(queries, keys_in)
        peak_score = jnp.max(scores, axis=-1, keepdims=True)
        log_total = peak_score + jnp.log(
            jnp.sum(jnp.exp(scores - peak_score), axis=-1, keepdims=True)
        )
        attention = jnp.exp(scores - log_total).astype(jnp.bfloat16).reshape(six_form)
        attended = jnp.einsum(
            "whabxy,xwyhc->awbhc", attention, values_in, preferred_element_type=jnp.float32
        )
        attended = attended.astype(jnp.bfloat16).reshape(row_count, inner_width)
        partial_proj = jnp.dot(attended, proj_full, preferred_element_type=jnp.float32)
        summed = lax.psum(partial_proj, "tp").reshape(WIN, grid_cols, full_width)
        hidden = token_grid + keep_cells * (summed + proj_bias)
        normed2, scaled2, inverse2 = norm_forward(hidden, ln2_gain, ln2_bias)
        entering2 = normed2.astype(jnp.bfloat16).reshape(row_count, full_width)
        preact = jnp.dot(entering2, fc1_full, preferred_element_type=jnp.float32) + fc1_bias
        activated = jax.nn.gelu(preact, approximate=False).astype(jnp.bfloat16)
        branch = jnp.dot(activated, fc2_full, preferred_element_type=jnp.float32).reshape(
            WIN, grid_cols, full_width
        )
        branch_local = summed_on_arrival(branch.astype(jnp.bfloat16), "tp", 2)
        hidden_local = lax.dynamic_slice_in_dim(hidden, local_start, local_width, 2)
        bias_local = lax.dynamic_slice_in_dim(fc2_bias, local_start, local_width, 0)
        result_part = (hidden_local + keep_cells * (branch_local + bias_local)).astype(jnp.bfloat16)
        qkv_back, proj_back, fc1_back, fc2_back = gathered
        cot_full = gathered_copies(cot_part, "tp", 2).astype(jnp.float32)
        masked = keep_cells * cot_full
        masked_low = masked.astype(jnp.bfloat16).reshape(row_count, full_width)
        grad_fc2 = jnp.einsum(
            "rf,rd->fd", activated, masked_low, preferred_element_type=jnp.float32
        )
        grad_fc2_bias = jnp.sum(masked, axis=(0, 1))
        grad_act = jnp.einsum("rd,fd->rf", masked_low, fc2_back, preferred_element_type=jnp.float32)
        slope_fn = jax.vjp(partial(jax.nn.gelu, approximate=False), preact)[1]
        grad_pre = slope_fn(grad_act)[0].astype(jnp.bfloat16)
        grad_fc1 = jnp.einsum("rd,rf->df", entering2, grad_pre, preferred_element_type=jnp.float32)
        grad_fc1_bias = jnp.sum(grad_pre.astype(jnp.float32), axis=0)
        norm2_terms = jnp.einsum(
            "rf,df->rd", grad_pre, fc1_back, preferred_element_type=jnp.float32
        )
        grad_norm2 = (
            lax.psum(norm2_terms.astype(jnp.bfloat16), "tp")
            .astype(jnp.float32)
            .reshape(WIN, grid_cols, full_width)
        )
        grad_ln2_gain = jnp.sum(grad_norm2 * scaled2, axis=(0, 1))
        grad_ln2_bias = jnp.sum(grad_norm2, axis=(0, 1))
        grad_hidden = cot_full + norm_backward(grad_norm2, scaled2, inverse2, ln2_gain)
        grad_branch = keep_cells * grad_hidden
        grad_proj_bias = jnp.sum(grad_branch, axis=(0, 1))
        branch_low = grad_branch.astype(jnp.bfloat16).reshape(row_count, full_width)
        grad_proj = jnp.einsum(
            "re,rd->ed", attended, branch_low, preferred_element_type=jnp.float32
        )
        grad_attended = jnp.einsum(
            "rd,ed->re", branch_low, proj_back, preferred_element_type=jnp.float32
        )
        grad_attended = grad_attended.astype(jnp.bfloat16).reshape(window_form)
        exact_soft = jnp.exp(score_block(queries, keys_in) - log_total)
        exact_low = exact_soft.astype(jnp.bfloat16).reshape(six_form)
        grad_values = jnp.einsum(
            "whabxy,awbhc->xwyhc", exact_low, grad_attended, preferred_element_type=jnp.float32
        ).astype(jnp.bfloat16)
        grad_soft = jnp.einsum(
            "awbhc,xwyhc->whabxy", grad_attended, values_in, preferred_element_type=jnp.float32
        )
        grad_soft = grad_soft.reshape(window_cols, heads_local, cell_count, cell_count)
        row_delta = jnp.sum(exact_soft * grad_soft, axis=-1, keepdims=True)
        grad_scores = (exact_soft * (grad_soft - row_delta)).astype(jnp.bfloat16).reshape(six_form)
        row_sums = jnp.sum(grad_scores.astype(jnp.float32), axis=5)
        col_sums = jnp.sum(grad_scores.astype(jnp.float32), axis=4)
        grad_queries = (
            jnp.einsum(
                "whabxy,xwyhc->awbhc", grad_scores, keys_in, preferred_element_type=jnp.float32
            )
            * scale_factor
        )
        grad_queries = grad_queries + jnp.einsum("whabx,axc->awbhc", row_sums, row_table)
        grad_queries = (grad_queries + jnp.einsum("whaby,byc->awbhc", col_sums, col_table)).astype(
            jnp.bfloat16
        )
        grad_keys = (
            jnp.einsum(
                "whabxy,awbhc->xwyhc", grad_scores, queries, preferred_element_type=jnp.float32
            )
            * scale_factor
        ).astype(jnp.bfloat16)
        query_exact = queries.astype(jnp.float32)
        row_full = jnp.einsum("awbhc,whabx->axc", query_exact, row_sums)
        col_full = jnp.einsum("awbhc,whaby->byc", query_exact, col_sums)
        grad_rows = jnp.einsum("axd,axc->dc", offsets, row_full)
        grad_cols = jnp.einsum("byd,byc->dc", offsets, col_full)
        stacked = jnp.stack(
            [
                grad_queries.reshape(row_count, inner_width),
                grad_keys.reshape(row_count, inner_width),
                grad_values.reshape(row_count, inner_width),
            ]
        )
        grad_qkv_bias = jnp.stack(
            [
                jnp.sum(stacked[0].astype(jnp.float32), axis=0),
                jnp.sum(stacked[2].astype(jnp.float32), axis=0),
            ]
        )
        grad_qkv = jnp.einsum("rd,tre->tde", entering, stacked, preferred_element_type=jnp.float32)
        norm1_terms = jnp.einsum(
            "tre,tde->rd", stacked, qkv_back, preferred_element_type=jnp.float32
        )
        grad_hidden_local = lax.dynamic_slice_in_dim(grad_hidden, local_start, local_width, 2)
        scaled1_local = lax.dynamic_slice_in_dim(scaled1, local_start, local_width, 2)
        share = summed_on_arrival(norm1_terms.astype(jnp.bfloat16), "tp", 1).reshape(
            WIN, grid_cols, local_width
        )
        norm1_local = keep_cells * share
        weighted = norm1_local * gain1_local
        first_total, second_total = in_one(
            (jnp.sum(weighted, axis=-1), jnp.sum(weighted * scaled1_local, axis=-1)), "tp"
        )
        first_mean = first_total[..., None] / full_width
        second_mean = second_total[..., None] / full_width
        grad_part = grad_hidden_local + inverse1 * (
            weighted - first_mean - scaled1_local * second_mean
        )
        grad_ln1_gain = lax.dynamic_update_slice_in_dim(
            zero_full, jnp.sum(norm1_local * scaled1_local, axis=(0, 1)), local_start, 0
        )
        grad_ln1_bias = lax.dynamic_update_slice_in_dim(
            zero_full, jnp.sum(norm1_local, axis=(0, 1)), local_start, 0
        )
        step_terms = (
            grad_ln1_gain,
            grad_ln1_bias,
            grad_qkv,
            grad_qkv_bias,
            grad_rows,
            grad_cols,
            grad_proj,
            grad_proj_bias,
            grad_ln2_gain,
            grad_ln2_bias,
            grad_fc1,
            grad_fc1_bias,
            grad_fc2,
            grad_fc2_bias,
        )
        totals = jax.tree.map(lambda earlier, update: earlier + update, totals, step_terms)
        return (totals, (result_part, grad_part))

    zero_totals = (
        jnp.zeros((full_width,), jnp.float32),
        jnp.zeros((full_width,), jnp.float32),
        jnp.zeros((3, full_width, inner_width), jnp.float32),
        jnp.zeros((2, inner_width), jnp.float32),
        jnp.zeros(rel_rows.shape, jnp.float32),
        jnp.zeros(rel_cols.shape, jnp.float32),
        jnp.zeros((inner_width, full_width), jnp.float32),
        jnp.zeros((full_width,), jnp.float32),
        jnp.zeros((full_width,), jnp.float32),
        jnp.zeros((full_width,), jnp.float32),
        jnp.zeros((full_width, hidden_width), jnp.float32),
        jnp.zeros((hidden_width,), jnp.float32),
        jnp.zeros((hidden_width, full_width), jnp.float32),
        jnp.zeros((full_width,), jnp.float32),
    )
    totals, outputs_all = lax.scan(micro_step, zero_totals, (tokens, valid_mask, cotangent))
    result_all, token_grads = outputs_all
    (
        sum_ln1_gain,
        sum_ln1_bias,
        sum_qkv,
        sum_qkv_bias,
        sum_rows,
        sum_cols,
        sum_proj,
        sum_proj_bias,
        sum_ln2_gain,
        sum_ln2_bias,
        sum_fc1,
        sum_fc1_bias,
        sum_fc2,
        sum_fc2_bias,
    ) = totals
    owned_part = (
        lax.psum_scatter(
            sum_qkv.astype(jnp.bfloat16), "shard", scatter_dimension=1, tiled=True
        ).astype(jnp.float32),
        lax.psum_scatter(
            sum_proj.astype(jnp.bfloat16), "shard", scatter_dimension=1, tiled=True
        ).astype(jnp.float32),
        lax.psum_scatter(
            sum_fc1.astype(jnp.bfloat16), "shard", scatter_dimension=0, tiled=True
        ).astype(jnp.float32),
        lax.psum_scatter(
            sum_fc2.astype(jnp.bfloat16), "shard", scatter_dimension=1, tiled=True
        ).astype(jnp.float32),
    )
    owned = (
        of_everyone(owned_part[0].astype(jnp.bfloat16), "ctx").astype(jnp.float32),
        of_everyone(owned_part[1].astype(jnp.bfloat16), "ctx").astype(jnp.float32),
        of_everyone(owned_part[2].astype(jnp.bfloat16), "ctx").astype(jnp.float32),
        of_everyone(owned_part[3].astype(jnp.bfloat16), "ctx").astype(jnp.float32),
    )
    heads_rows, heads_cols, heads_gain, heads_bias = in_one(
        (sum_rows, sum_cols, sum_ln1_gain, sum_ln1_bias), "tp"
    )
    small_all = (
        of_everyone(heads_gain.astype(jnp.bfloat16), ("shard", "ctx")).astype(jnp.float32),
        of_everyone(heads_bias.astype(jnp.bfloat16), ("shard", "ctx")).astype(jnp.float32),
        of_everyone(sum_qkv_bias.astype(jnp.bfloat16), ("shard", "ctx")).astype(jnp.float32),
        of_everyone(heads_rows.astype(jnp.bfloat16), ("shard", "ctx")).astype(jnp.float32),
        of_everyone(heads_cols.astype(jnp.bfloat16), ("shard", "ctx")).astype(jnp.float32),
        of_everyone(sum_proj_bias.astype(jnp.bfloat16), ("shard", "ctx")).astype(jnp.float32),
        of_everyone(sum_ln2_gain.astype(jnp.bfloat16), ("shard", "ctx")).astype(jnp.float32),
        of_everyone(sum_ln2_bias.astype(jnp.bfloat16), ("shard", "ctx")).astype(jnp.float32),
        of_everyone(sum_fc1_bias.astype(jnp.bfloat16), ("shard", "ctx")).astype(jnp.float32),
        of_everyone(sum_fc2_bias.astype(jnp.bfloat16), ("shard", "ctx")).astype(jnp.float32),
    )
    return (
        result_all,
        token_grads,
        small_all[0],
        small_all[1],
        owned[0],
        small_all[2],
        small_all[3],
        small_all[4],
        owned[1],
        small_all[5],
        small_all[6],
        small_all[7],
        owned[2],
        small_all[8],
        owned[3],
        small_all[9],
    )


def solution(mesh):
    in_specs = (
        P("shard", "ctx", None, "tp"),
        P("shard", "ctx", None),
        P(),
        P(),
        P(None, "shard", "tp"),
        P(None, "tp"),
        P(),
        P(),
        P("tp", "shard"),
        P(),
        P(),
        P(),
        P("shard", "tp"),
        P("tp"),
        P("tp", "shard"),
        P(),
        P("shard", "ctx", None, "tp"),
    )
    out_specs = (
        P("shard", "ctx", None, "tp"),
        P("shard", "ctx", None, "tp"),
        P(),
        P(),
        P(None, "shard", "tp"),
        P(None, "tp"),
        P(),
        P(),
        P("tp", "shard"),
        P(),
        P(),
        P(),
        P("shard", "tp"),
        P("tp"),
        P("tp", "shard"),
        P(),
    )
    return jax.shard_map(local, mesh=mesh, in_specs=in_specs, out_specs=out_specs, check_vma=False)
```

profile of v0, /device:TPU:0, one launch (start us, length us, event | category | flops | bytes accessed | tf_op | source)
XLA Modules:
  0.0 1321.8 jit_solution(15659164494034461880)
XLA Ops:
  19.9 1013.4 %while.45 = (s32[]{:T(128)}, f32[1280]{0:T(1024)}, f32[1280]{0:T(1024)}, f32[3,1280,320]{1,2,0:T(8,128)}, f32[2,320]{1,0:T(2,128)}, /*index=5*/f32[27,80]{1,0:T(...) while((s32[]{:T(128)}, f32[1280]{0:T(1024)}, ...), condition=%wide.wide.region_28.29_spmd.clone.clone, body=%wide.wide.region_0.28_spmd.clone.clone.sunk | while | flops 17979088896 | bytes 544991104 | solution.py:338
  29.3 25.0 %all-to-all-done.1 = bf16[4,14,42,320]{3,2,1,0:T(8,128)(2,1)S(1)} async-done(((bf16[4,14,42,320]{3,2,1,0:T(8,128)(2,1)}), bf16[4,14,42,320]{3,2,1,0:T(8,128)(2,1)S(1)}, u32[]{:S(2)}, u32[]{:S(2)}) %all-to-all-start.1) | async-done | bytes 1505312 | tf_op jit(solution)/shard_map/while/body/eval_jaxpr/all_to_all | solution.py:32
  65.9 18.6 %all-gather.2.cloned.1.call-done = bf16[1280,3840]{1,0:T(8,128)(2,1)} async-done(((bf16[80,3840]{1,0:T(8,128)(2,1)}), bf16[1280,3840]{1,0:T(8,128)(2,1)}) %all-gather.2.cloned.1.call-update) | async-done | bytes 9830416 | tf_op jit(solution)/shard_map/while/body/eval_jaxpr/all_gather | solution.py:20
  123.3 19.7 %fusion.289 = (f32[3,4,14,14]{3,2,1,0:T(8,128)S(1)}, f32[3,4,14,14,14,14]{3,5,4,2,1,0:T(8,128)}) fusion(f32[3,4,14,14,14]{3,4,2,1,0:T(8,128)} %copy.663, f32[3,4,14,14,14]{3,4,2,1,0:T(8,128)} %copy.664, bf16[14,3,14,4,80,1]{4,3,2,1,0,5:T(4,128)(2,1)S(1)} %bitcast.363, bf16[14,3,14,4,80,1]{4,3,2,1,0,5:T(4,128)(2,1)S(1)} %copy-done.16), kind=kOutput, calls=%fused_computation.204.clone.clone.1 | convolution fusion | flops 75600336 | bytes 2869440 | tf_op jit(solution)/shard_map/while/body/eval_jaxpr/awbhc,xwyhc->whabxy/dot_general | solution.py:143
  142.9 12.2 exponential_reduce_fusion.3
  156.7 9.4 fusion.290
  180.7 48.1 %all-to-all-done = bf16[4,14,42,320]{3,2,1,0:T(8,128)(2,1)} async-done(((bf16[4,14,42,320]{3,2,1,0:T(8,128)(2,1)}), bf16[4,14,42,320]{3,2,1,0:T(8,128)(2,1)}, u32[]{:S(2)}, u32[]{:S(2)}) %all-to-all-start) | async-done | bytes 1505312 | tf_op jit(solution)/shard_map/while/body/eval_jaxpr/all_to_all | solution.py:32
  251.5 17.1 %all-reduce.3.cloned.1.call-done = f32[588,1280]{1,0:T(8,128)} async-done(((f32[588,1280]{1,0:T(8,128)}), f32[588,1280]{1,0:T(8,128)}) %all-reduce.3.cloned.1.call-update) | async-done | bytes 3010576 | tf_op jit(solution)/shard_map/while/body/eval_jaxpr/psum | solution.py:184
  284.2 12.5 multiply_convert_fusion.15
  322.6 7.9 convolution_add_fusion.11
  344.3 11.8 all-to-all-done.3
  376.1 11.4 convert_reduce_fusion.35
  387.5 13.0 multiply_reduce_fusion.28
  400.5 17.3 %convert_reduce_fusion.36 = (bf16[3,4,14,14,14]{3,4,2,1,0:T(8,128)(2,1)}, bf16[3,4,14,14,14]{3,4,2,1,0:T(8,128)(2,1)S(1)}, bf16[3,4,14,14,14,14]{3,5,4,2,1,0:T(8,128)(2,1)S(1)}) fusion(f32[3,4,14,14,14,14]{3,5,4,2,1,0:T(8,128)} %get-tuple-element.1618, f32[3,4,14,14]{3,2,1,0:T(8,128)S(1)} %get-tuple-element.1619, ...), kind=kLoop, calls=%fused_computation.2.clone.clone.1 | loop fusion | flops 3161088 | bytes 4760448 | tf_op jit(solution)/shard_map/while/body/eval_jaxpr/reduce_sum | solution.py:242
  438.3 6.8 multiply_reduce_fusion.31
  477.7 8.1 all-to-all-done.2
  505.2 18.8 %dynamic_update_slice.37 = f32[2,14,42,320]{3,0,2,1:T(2,128)} dynamic-update-slice(f32[2,14,42,320]{3,0,2,1:T(2,128)} %get-tuple-element.1701, f32[1,14,42,320]{3,0,2,1:T(1,128)S(1)} %copy.679, s32[]{:T(128)S(6)} %copy.703, s32[]{:T(128)} %constant.203.clone.1..sunk, s32[]{:T(128)} %constant.203.clone.1..sunk, s32[]{:T(128)} %constant.203.clone.1..sunk) | dynamic-update-slice | bytes 1505284 | tf_op jit(solution)/shard_map/while/body/jit(dynamic_update_index_in_dim)/dynamic_update_slice | solution.py:338
  532.5 23.4 %all-to-all-done.1 = bf16[4,14,42,320]{3,2,1,0:T(8,128)(2,1)S(1)} async-done(((bf16[4,14,42,320]{3,2,1,0:T(8,128)(2,1)}), bf16[4,14,42,320]{3,2,1,0:T(8,128)(2,1)S(1)}, u32[]{:S(2)}, u32[]{:S(2)}) %all-to-all-start.1) | async-done | bytes 1505312 | tf_op jit(solution)/shard_map/while/body/eval_jaxpr/all_to_all | solution.py:32
  567.6 17.5 %all-gather.2.cloned.1.call-done = bf16[1280,3840]{1,0:T(8,128)(2,1)} async-done(((bf16[80,3840]{1,0:T(8,128)(2,1)}), bf16[1280,3840]{1,0:T(8,128)(2,1)}) %all-gather.2.cloned.1.call-update) | async-done | bytes 9830416 | tf_op jit(solution)/shard_map/while/body/eval_jaxpr/all_gather | solution.py:20
  623.8 19.7 %fusion.289 = (f32[3,4,14,14]{3,2,1,0:T(8,128)S(1)}, f32[3,4,14,14,14,14]{3,5,4,2,1,0:T(8,128)}) fusion(f32[3,4,14,14,14]{3,4,2,1,0:T(8,128)} %copy.663, f32[3,4,14,14,14]{3,4,2,1,0:T(8,128)} %copy.664, bf16[14,3,14,4,80,1]{4,3,2,1,0,5:T(4,128)(2,1)S(1)} %bitcast.363, bf16[14,3,14,4,80,1]{4,3,2,1,0,5:T(4,128)(2,1)S(1)} %copy-done.16), kind=kOutput, calls=%fused_computation.204.clone.clone.1 | convolution fusion | flops 75600336 | bytes 2869440 | tf_op jit(solution)/shard_map/while/body/eval_jaxpr/awbhc,xwyhc->whabxy/dot_general | solution.py:143
  643.5 12.2 exponential_reduce_fusion.3
  657.2 9.4 fusion.290
  681.3 48.1 %all-to-all-done = bf16[4,14,42,320]{3,2,1,0:T(8,128)(2,1)} async-done(((bf16[4,14,42,320]{3,2,1,0:T(8,128)(2,1)}), bf16[4,14,42,320]{3,2,1,0:T(8,128)(2,1)}, u32[]{:S(2)}, u32[]{:S(2)}) %all-to-all-start) | async-done | bytes 1505312 | tf_op jit(solution)/shard_map/while/body/eval_jaxpr/all_to_all | solution.py:32
  752.1 17.1 %all-reduce.3.cloned.1.call-done = f32[588,1280]{1,0:T(8,128)} async-done(((f32[588,1280]{1,0:T(8,128)}), f32[588,1280]{1,0:T(8,128)}) %all-reduce.3.cloned.1.call-update) | async-done | bytes 3010576 | tf_op jit(solution)/shard_map/while/body/eval_jaxpr/psum | solution.py:184
  784.8 12.5 multiply_convert_fusion.15
  823.2 9.9 convolution_add_fusion.11
  833.1 6.8 convolution_add_fusion.12
  848.6 8.1 all-to-all-done.3
  876.7 11.4 convert_reduce_fusion.35
  888.1 13.0 multiply_reduce_fusion.28
  901.0 17.3 %convert_reduce_fusion.36 = (bf16[3,4,14,14,14]{3,4,2,1,0:T(8,128)(2,1)}, bf16[3,4,14,14,14]{3,4,2,1,0:T(8,128)(2,1)S(1)}, bf16[3,4,14,14,14,14]{3,5,4,2,1,0:T(8,128)(2,1)S(1)}) fusion(f32[3,4,14,14,14,14]{3,5,4,2,1,0:T(8,128)} %get-tuple-element.1618, f32[3,4,14,14]{3,2,1,0:T(8,128)S(1)} %get-tuple-element.1619, ...), kind=kLoop, calls=%fused_computation.2.clone.clone.1 | loop fusion | flops 3161088 | bytes 4760448 | tf_op jit(solution)/shard_map/while/body/eval_jaxpr/reduce_sum | solution.py:242
  938.9 6.8 multiply_reduce_fusion.31
  973.5 7.0 bitcast_add_fusion.3
  980.5 5.9 all-to-all-done.2
  1005.8 18.8 %dynamic_update_slice.37 = f32[2,14,42,320]{3,0,2,1:T(2,128)} dynamic-update-slice(f32[2,14,42,320]{3,0,2,1:T(2,128)} %get-tuple-element.1701, f32[1,14,42,320]{3,0,2,1:T(1,128)S(1)} %copy.679, s32[]{:T(128)S(6)} %copy.703, s32[]{:T(128)} %constant.203.clone.1..sunk, s32[]{:T(128)} %constant.203.clone.1..sunk, s32[]{:T(128)} %constant.203.clone.1..sunk) | dynamic-update-slice | bytes 1505284 | tf_op jit(solution)/shard_map/while/body/jit(dynamic_update_index_in_dim)/dynamic_update_slice | solution.py:338
  1040.4 7.6 copy.425
  1048.0 8.3 reshape.619
  1073.3 7.3 all-to-all-start.9
  1093.8 5.7 all-to-all-done.19
  1115.2 7.3 all-to-all-done.15
  1137.9 6.7 all-to-all-done.14
  1150.4 5.7 all-to-all-done.13
  1171.7 7.7 all-to-all-done.6
  1185.7 8.2 all-to-all-done.10
  1200.4 8.1 all-to-all-done.11
  1226.3 7.5 all-to-all-done.8
  1240.4 59.4 %reduce-scatter.17.cloned.1.call-done = bf16[80,1280]{1,0:T(8,128)(2,1)} async-done(((bf16[1280,1280]{1,0:T(8,128)(2,1)}), bf16[80,1280]{1,0:T(8,128)(2,1)}) %reduce-scatter.17.cloned.1.call-update) | async-done | bytes 204816
  1307.2 5.9 all-to-all-done.18
  (727 shorter events, 625.2 us)
Async XLA Ops:
  20.4 92.9 %copy-start.32 = (bf16[14,14,80]{2,1,0:T(8,128)(2,1)}, bf16[14,14,80]{2,1,0:T(8,128)(2,1)S(1)}, u32[]{:S(2)}) copy-start(bf16[14,14,80]{2,1,0:T(8,128)(2,1)S(1)} %get-tuple-element.1757) | copy-start | bytes 94084 | tf_op jit(solution)/shard_map/while
  20.4 97.8 %copy-start.30 = (bf16[14,14,80]{2,1,0:T(8,128)(2,1)}, bf16[14,14,80]{2,1,0:T(8,128)(2,1)S(1)}, u32[]{:S(2)}) copy-start(bf16[14,14,80]{2,1,0:T(8,128)(2,1)S(1)} %get-tuple-element.1758) | copy-start | bytes 94084 | tf_op jit(solution)/shard_map/while
  20.4 337.9 %copy-start.74 = (f32[320]{0:T(512)}, f32[320]{0:T(512)S(1)}, u32[]{:S(2)}) copy-start(f32[320]{0:T(512)S(1)} %get-tuple-element.1759) | copy-start | bytes 3844 | tf_op jit(solution)/shard_map/while
  20.4 64.1 %all-gather.2.cloned.1.call-start = ((), (), s32[]{:S(2)}) async-start(), calls=%async_computation.28 | async-start | bytes 10444800 | tf_op jit(solution)/shard_map/while/body/eval_jaxpr/all_gather | solution.py:20
  23.9 30.4 %all-to-all-start.1 = ((bf16[4,14,42,320]{3,2,1,0:T(8,128)(2,1)}), bf16[4,14,42,320]{3,2,1,0:T(8,128)(2,1)S(1)}, u32[]{:S(2)}, u32[]{:S(2)}) async-start(bf16[4,14,42,320]{3,2,1,0:T(8,128)(2,1)} %broadcast_in_dim.214), calls=%async_computation.1 | async-start | bytes 4128768 | tf_op jit(solution)/shard_map/while/body/eval_jaxpr/all_to_all | solution.py:32
  28.3 240.4 %all-reduce.3.cloned.1.call-start = ((), (), s32[]{:S(2)}) async-start(), calls=%async_computation.29 | async-start | bytes 6062080 | tf_op jit(solution)/shard_map/while/body/eval_jaxpr/psum | solution.py:184
  175.5 53.3 %all-to-all-start = ((bf16[4,14,42,320]{3,2,1,0:T(8,128)(2,1)}), bf16[4,14,42,320]{3,2,1,0:T(8,128)(2,1)}, u32[]{:S(2)}, u32[]{:S(2)}) async-start(bf16[4,14,42,320]{3,2,1,0:T(8,128)(2,1)} %broadcast_in_dim.213), calls=%async_computation | async-start | bytes 4128768 | tf_op jit(solution)/shard_map/while/body/eval_jaxpr/all_to_all | solution.py:32
  180.0 182.7 %all-reduce.5.cloned.1.call-start = ((), (), s32[]{:S(2)}) async-start(), calls=%async_computation.30 | async-start | bytes 3031040 | tf_op jit(solution)/shard_map/while/body/eval_jaxpr/psum | solution.py:214
  318.0 38.2 %all-to-all-start.3 = ((bf16[4,14,42,320]{3,2,1,0:T(8,128)(2,1)}), bf16[4,14,42,320]{3,2,1,0:T(8,128)(2,1)}, u32[]{:S(2)}, u32[]{:S(2)}) async-start(bf16[4,14,42,320]{3,2,1,0:T(8,128)(2,1)} %bitcast.359), calls=%async_computation.3 | async-start | bytes 4128768 | tf_op jit(solution)/shard_map/while/body/eval_jaxpr/all_to_all | solution.py:55
  459.2 26.6 %all-to-all-start.2 = ((bf16[4,588,320]{1,2,0:T(8,128)(2,1)}), bf16[4,588,320]{1,2,0:T(8,128)(2,1)}, u32[]{:S(2)}, u32[]{:S(2)}) async-start(bf16[4,588,320]{1,2,0:T(8,128)(2,1)} %bitcast.360), calls=%async_computation.2 | async-start | bytes 3276800 | tf_op jit(solution)/shard_map/while/body/eval_jaxpr/all_to_all | solution.py:55
  491.4 8.6 all-to-all-start.4
  524.3 89.5 %copy-start.32 = (bf16[14,14,80]{2,1,0:T(8,128)(2,1)}, bf16[14,14,80]{2,1,0:T(8,128)(2,1)S(1)}, u32[]{:S(2)}) copy-start(bf16[14,14,80]{2,1,0:T(8,128)(2,1)S(1)} %get-tuple-element.1757) | copy-start | bytes 94084 | tf_op jit(solution)/shard_map/while
  524.3 94.5 %copy-start.30 = (bf16[14,14,80]{2,1,0:T(8,128)(2,1)}, bf16[14,14,80]{2,1,0:T(8,128)(2,1)S(1)}, u32[]{:S(2)}) copy-start(bf16[14,14,80]{2,1,0:T(8,128)(2,1)S(1)} %get-tuple-element.1758) | copy-start | bytes 94084 | tf_op jit(solution)/shard_map/while
  524.3 334.5 %copy-start.74 = (f32[320]{0:T(512)}, f32[320]{0:T(512)S(1)}, u32[]{:S(2)}) copy-start(f32[320]{0:T(512)S(1)} %get-tuple-element.1759) | copy-start | bytes 3844 | tf_op jit(solution)/shard_map/while
  524.3 60.7 %all-gather.2.cloned.1.call-start = ((), (), s32[]{:S(2)}) async-start(), calls=%async_computation.28 | async-start | bytes 10444800 | tf_op jit(solution)/shard_map/while/body/eval_jaxpr/all_gather | solution.py:20
  527.8 28.1 %all-to-all-start.1 = ((bf16[4,14,42,320]{3,2,1,0:T(8,128)(2,1)}), bf16[4,14,42,320]{3,2,1,0:T(8,128)(2,1)S(1)}, u32[]{:S(2)}, u32[]{:S(2)}) async-start(bf16[4,14,42,320]{3,2,1,0:T(8,128)(2,1)} %broadcast_in_dim.214), calls=%async_computation.1 | async-start | bytes 4128768 | tf_op jit(solution)/shard_map/while/body/eval_jaxpr/all_to_all | solution.py:32
  531.4 237.8 %all-reduce.3.cloned.1.call-start = ((), (), s32[]{:S(2)}) async-start(), calls=%async_computation.29 | async-start | bytes 6062080 | tf_op jit(solution)/shard_map/while/body/eval_jaxpr/psum | solution.py:184
  676.1 53.3 %all-to-all-start = ((bf16[4,14,42,320]{3,2,1,0:T(8,128)(2,1)}), bf16[4,14,42,320]{3,2,1,0:T(8,128)(2,1)}, u32[]{:S(2)}, u32[]{:S(2)}) async-start(bf16[4,14,42,320]{3,2,1,0:T(8,128)(2,1)} %broadcast_in_dim.213), calls=%async_computation | async-start | bytes 4128768 | tf_op jit(solution)/shard_map/while/body/eval_jaxpr/all_to_all | solution.py:32
  680.6 182.7 %all-reduce.5.cloned.1.call-start = ((), (), s32[]{:S(2)}) async-start(), calls=%async_computation.30 | async-start | bytes 3031040 | tf_op jit(solution)/shard_map/while/body/eval_jaxpr/psum | solution.py:214
  818.5 38.2 %all-to-all-start.3 = ((bf16[4,14,42,320]{3,2,1,0:T(8,128)(2,1)}), bf16[4,14,42,320]{3,2,1,0:T(8,128)(2,1)}, u32[]{:S(2)}, u32[]{:S(2)}) async-start(bf16[4,14,42,320]{3,2,1,0:T(8,128)(2,1)} %bitcast.359), calls=%async_computation.3 | async-start | bytes 4128768 | tf_op jit(solution)/shard_map/while/body/eval_jaxpr/all_to_all | solution.py:55
  959.8 26.6 %all-to-all-start.2 = ((bf16[4,588,320]{1,2,0:T(8,128)(2,1)}), bf16[4,588,320]{1,2,0:T(8,128)(2,1)}, u32[]{:S(2)}, u32[]{:S(2)}) async-start(bf16[4,588,320]{1,2,0:T(8,128)(2,1)} %bitcast.360), calls=%async_computation.2 | async-start | bytes 3276800 | tf_op jit(solution)/shard_map/while/body/eval_jaxpr/all_to_all | solution.py:55
  991.9 8.6 all-to-all-start.4
  1033.3 175.3 %reduce-scatter.15.cloned.1.call-start = ((), (), s32[]{:S(2)}) async-start(), calls=%async_computation.26 | async-start | bytes 1044480
  1036.2 177.9 %reduce-scatter.13.cloned.1.call-start = ((), (), s32[]{:S(2)}) async-start(), calls=%async_computation.25 | async-start | bytes 2785280
  1056.3 177.5 %reduce-scatter.11.cloned.1.call-start = ((), (), s32[]{:S(2)}) async-start(), calls=%async_computation.24 | async-start | bytes 3481600 | tf_op jit(solution)/shard_map/reduce_scatter | solution.py:363
  1061.3 238.5 %reduce-scatter.17.cloned.1.call-start = ((), (), s32[]{:S(2)}) async-start(), calls=%async_computation.27 | async-start | bytes 3481600
  1071.9 43.0 %copy-start.82 = (f32[27,80]{1,0:T(8,128)S(1)}, f32[27,80]{1,0:T(8,128)}, u32[]{:S(2)}) copy-start(f32[27,80]{1,0:T(8,128)} %get-tuple-element.1954) | copy-start | bytes 25924
  1071.9 43.0 %copy-start.79 = (f32[27,80]{1,0:T(8,128)S(1)}, f32[27,80]{1,0:T(8,128)}, u32[]{:S(2)}) copy-start(f32[27,80]{1,0:T(8,128)} %get-tuple-element.1955) | copy-start | bytes 25924
  1072.0 43.1 %copy-start.70 = (f32[1280]{0:T(1024)S(1)}, f32[1280]{0:T(1024)}, u32[]{:S(2)}) copy-start(f32[1280]{0:T(1024)} %get-tuple-element.1951) | copy-start | bytes 15364
  1072.0 43.1 %copy-start.71 = (f32[1280]{0:T(1024)S(1)}, f32[1280]{0:T(1024)}, u32[]{:S(2)}) copy-start(f32[1280]{0:T(1024)} %get-tuple-element.1950) | copy-start | bytes 15364
  1072.0 54.6 %copy-start.55 = (f32[1280]{0:T(1024)S(1)}, f32[1280]{0:T(1024)}, u32[]{:S(2)}) copy-start(f32[1280]{0:T(1024)} %get-tuple-element.1957) | copy-start | bytes 15364
  1072.0 54.6 %copy-start.52 = (f32[1280]{0:T(1024)S(1)}, f32[1280]{0:T(1024)}, u32[]{:S(2)}) copy-start(f32[1280]{0:T(1024)} %get-tuple-element.1958) | copy-start | bytes 15364
  1073.3 14.8 %all-to-all-start.9 = ((bf16[32,2,320]{2,1,0:T(2,128)(2,1)}), bf16[32,2,320]{2,1,0:T(2,128)(2,1)S(1)}, u32[]{:S(2)}, u32[]{:S(2)}) async-start(bf16[32,2,320]{2,1,0:T(2,128)(2,1)} %broadcast_in_dim.114), calls=%async_computation.9 | async-start | bytes 98304 | tf_op jit(solution)/shard_map/all_to_all | solution.py:32
  1088.1 11.5 all-to-all-start.19
  1099.6 11.5 all-to-all-start.17
  1111.0 11.5 all-to-all-start.15
  1123.2 9.9 all-to-all-start.5
  1133.1 11.5 all-to-all-start.14
  1144.6 11.6 all-to-all-start.13
  1156.2 11.5 all-to-all-start.7
  1167.6 11.7 all-to-all-start.6
  1180.1 13.8 %all-to-all-start.10 = ((bf16[32,27,80]{2,1,0:T(8,128)(2,1)}), bf16[32,27,80]{2,1,0:T(8,128)(2,1)S(1)}, u32[]{:S(2)}, u32[]{:S(2)}) async-start(bf16[32,27,80]{2,1,0:T(8,128)(2,1)} %broadcast_in_dim.115), calls=%async_computation.10 | async-start | bytes 524288 | tf_op jit(solution)/shard_map/all_to_all | solution.py:32
  1194.7 13.9 %all-to-all-start.11 = ((bf16[32,27,80]{2,1,0:T(8,128)(2,1)}), bf16[32,27,80]{2,1,0:T(8,128)(2,1)S(1)}, u32[]{:S(2)}, u32[]{:S(2)}) async-start(bf16[32,27,80]{2,1,0:T(8,128)(2,1)} %broadcast_in_dim.116), calls=%async_computation.11 | async-start | bytes 524288 | tf_op jit(solution)/shard_map/all_to_all | solution.py:32
  1210.1 10.7 all-to-all-start.12
  1221.5 12.3 all-to-all-start.8
  1225.0 88.9 %copy-start.1 = (bf16[27,80]{1,0:T(8,128)(2,1)S(1)}, bf16[27,80]{1,0:T(8,128)(2,1)}, u32[]{:S(2)}) copy-start(bf16[27,80]{1,0:T(8,128)(2,1)} %param.26) | copy-start | bytes 12964
  1235.5 64.3 %all-to-all-start.16 = ((bf16[2,80,1280]{2,1,0:T(8,128)(2,1)}), bf16[2,80,1280]{2,1,0:T(8,128)(2,1)S(1)}, u32[]{:S(2)}, u32[]{:S(2)}) async-start(bf16[2,80,1280]{2,1,0:T(8,128)(2,1)} %broadcast_in_dim.121), calls=%async_computation.17 | async-start | bytes 819200 | tf_op jit(solution)/shard_map/all_to_all | solution.py:32
  1301.5 11.6 all-to-all-start.18
  (151 other events, 1346.7 us)
Sparse Core Ops, SparseCore 0:
  23.0 61.4 all-gather.1
  173.0 95.6 all-reduce.2
  304.4 58.2 all-reduce.4
  526.7 58.3 all-gather.1
  673.6 95.6 all-reduce.2
  804.9 58.2 all-reduce.4
Sparse Core Ops, SparseCore 1:
  1036.3 61.1 reduce-scatter.14
  1099.9 63.6 reduce-scatter.12
  1166.0 66.3 reduce-scatter.10
  1234.9 64.8 reduce-scatter.16
where the time goes:
time: 1330 us; the launch traced here: 1320 us
  waiting for transfers between devices  404 us (30%)
  local copies, waits for them, and re-layouts  324 us (24%)
  matrix products  269 us (20%)
  other arithmetic  193 us (15%)
  starting transfers between devices  103 us (8%)
  between operations  16.7 us (1%)
    all_to_all x21, waiting for transfers between devices, from_everyone(): lax.all_to_all(jnp.broadcast_to(array[None], (size, *array.shape)), axis,...  237 us
    all_to_all x21, starting transfers between devices, from_everyone(): lax.all_to_all(jnp.broadcast_to(array[None], (size, *array.shape)), axis,...  83.9 us
    unnamed x7, waiting for transfers between devices  59.5 us
    dynamic_update_slice x4, local copies, waits for them, and re-layouts, local(): lax.scan(micro_step, zero_totals, (tokens, valid_mask, cotangent))  39.4 us
    dot_general x2, matrix products, score_block(): jnp.einsum('awbhc,xwyhc->whabxy', query_win, key_win, preferred_element_t...  39.3 us
    all_gather x2, waiting for transfers between devices, rows_first(): out = lax.all_gather(both, axis, axis=0, tiled=True)  36.1 us
    unnamed x66, local copies, waits for them, and re-layouts  35.9 us
    reduce_sum x2, other arithmetic, micro_step(): row_sums = jnp.sum(grad_scores.astype(jnp.float32), axis=5)  34.6 us
  transfers between devices with their start and end apart: 35, of which 30 were waited for; matrix products, arithmetic and copies ran while one was open for 20% of the time, Pallas kernels for 0%

commit v1 on v0

v1 whole, which is shorter than its diff:
```python
import jax
import jax.numpy as jnp
import numpy as np
from jax import lax
from jax.experimental import pallas as pl
from jax.experimental.pallas import tpu as pltpu
from jax.sharding import PartitionSpec as P

HEADS = 16
HDIM = 80
WIN = 14
D = 1280
NT = 4
HL = HEADS // NT
CELLS = WIN * WIN
WR = 208
NW = 6
TS = 320
HALF = TS // 2
HP = 128
RELS = 2 * WIN - 1
EPS = 1e-06
SCALE = HDIM ** (-0.5)
bf = jnp.bfloat16
f32 = jnp.float32
VM = 60 * 1024 * 1024


def rel_constants():
    sel = np.zeros((512, 64), np.float32)
    mask = np.zeros((WR, 512), np.float32)
    spread = np.zeros((512, WR), np.float32)
    for a in range(WIN):
        for x in range(WIN):
            sel[a * WIN + x, a - x + WIN - 1] = 1
            sel[256 + a * WIN + x, 32 + a - x + WIN - 1] = 1
    for a in range(WIN):
        for b in range(WIN):
            row = a * WIN + b
            mask[row, a * WIN : a * WIN + WIN] = 1
            mask[row, 256 + b * WIN : 256 + b * WIN + WIN] = 1
    for a in range(WIN):
        for x in range(WIN):
            for y in range(WIN):
                spread[a * WIN + x, x * WIN + y] = 1
                spread[256 + a * WIN + y, x * WIN + y] = 1
    keys = np.where(np.arange(WR) < CELLS, 0.0, -1e30).astype(np.float32)[None]
    return sel, mask, spread, keys


def dot(a, b):
    return lax.dot_general(a, b, (((1,), (0,)), ((), ())), preferred_element_type=f32)


def dot_nt(a, b):
    return lax.dot_general(a, b, (((1,), (1,)), ((), ())), preferred_element_type=f32)


def dot_tn(a, b):
    return lax.dot_general(a, b, (((0,), (0,)), ((), ())), preferred_element_type=f32)


def params():
    return pltpu.CompilerParams(vmem_limit_bytes=VM)


def cost(flops, nbytes, trans=0):
    return pl.CostEstimate(flops=int(flops), bytes_accessed=int(nbytes), transcendentals=int(trans))


def sds(shape, dtype):
    return jax.ShapeDtypeStruct(shape, dtype)


def full(shape):
    return pl.BlockSpec(shape, lambda *g: (0,) * len(shape))


ANY = pl.BlockSpec(memory_space=pl.ANY)


def stats(x):
    mean = jnp.sum(x, axis=1, keepdims=True) * (1.0 / D)
    xc = x - mean
    var = jnp.sum(xc * xc, axis=1, keepdims=True) * (1.0 / D)
    inv = lax.rsqrt(var + EPS)
    return xc * inv, inv


def colsum(x):
    return jnp.sum(x, axis=0, keepdims=True)


def acc_out(ref, value):
    @pl.when(pl.program_id(0) == 0)
    def _():
        ref[...] = jnp.zeros_like(ref)

    ref[...] += value


RB = 80


def ln1_body(tok_ref, cot_ref, keep_ref, g_ref, b_ref, x_ref, c_ref, e_ref, gb_ref, fb_ref):
    keep = keep_ref[...]
    x = jnp.concatenate([tok_ref[k].astype(f32) for k in range(NT)], axis=1)
    c = jnp.concatenate([cot_ref[k].astype(f32) for k in range(NT)], axis=1)
    n, _ = stats(x)
    e_ref[...] = (keep * (n * g_ref[...] + b_ref[...])).astype(bf)
    x_ref[...] = x.astype(bf)
    c_ref[...] = c.astype(bf)
    gb = keep * c
    gb_ref[...] = gb.astype(bf)
    acc_out(fb_ref, colsum(gb))


def ln1_call(tok4, cot4, keep, g, b):
    blk = pl.BlockSpec((NT, RB, TS), lambda i: (0, i, 0))
    row = pl.BlockSpec((RB, D), lambda i: (i, 0))
    kp = pl.BlockSpec((RB, 1), lambda i: (i, 0))
    return pl.pallas_call(
        ln1_body,
        grid=(TS // RB,),
        in_specs=[blk, blk, kp, full((1, D)), full((1, D))],
        out_specs=[row, row, row, row, full((1, D))],
        out_shape=[sds((TS, D), bf)] * 4 + [sds((1, D), f32)],
        compiler_params=params(),
        cost_estimate=cost(30 * TS * D, 14 * TS * D),
        name="ln1",
    )(tok4, cot4, keep, g, b)


def ln2_body(r0, c1, c3, x, keep, pb, g, b, h_ref, e_ref):
    s = r0[...] + c1[...].astype(f32) + c3[...].astype(f32)
    h = x[...].astype(f32) + keep[...] * (s + pb[...])
    h_ref[...] = h
    n, _ = stats(h)
    e_ref[...] = (n * g[...] + b[...]).astype(bf)


def ln2_call(r0, c1, c3, x, keep, pb, g, b):
    row = pl.BlockSpec((RB, D), lambda i: (i, 0))
    kp = pl.BlockSpec((RB, 1), lambda i: (i, 0))
    return pl.pallas_call(
        ln2_body,
        grid=(TS // RB,),
        in_specs=[row, row, row, row, kp] + [full((1, D))] * 3,
        out_specs=[row, row],
        out_shape=[sds((TS, D), f32), sds((TS, D), bf)],
        compiler_params=params(),
        cost_estimate=cost(20 * TS * D, 16 * TS * D),
        name="ln2",
    )(r0, c1, c3, x, keep, pb, g, b)


def result_body(r0, c1, c3, h, keep, fb, o_ref):
    s = r0[...] + c1[...].astype(f32) + c3[...].astype(f32)
    o = (h[...] + keep[...] * (s + fb[...])).astype(bf)
    for k in range(NT):
        o_ref[k] = o[:, k * TS : (k + 1) * TS]


def result_call(r0, c1, c3, h, keep, fb):
    row = pl.BlockSpec((RB, D), lambda i: (i, 0))
    kp = pl.BlockSpec((RB, 1), lambda i: (i, 0))
    return pl.pallas_call(
        result_body,
        grid=(TS // RB,),
        in_specs=[row, row, row, row, kp, full((1, D))],
        out_specs=pl.BlockSpec((NT, RB, TS), lambda i: (0, i, 0)),
        out_shape=sds((NT, TS, TS), bf),
        compiler_params=params(),
        cost_estimate=cost(8 * TS * D, 14 * TS * D),
        name="result",
    )(r0, c1, c3, h, keep, fb)


def norm_back(w, n, inv):
    m1 = jnp.sum(w, axis=1, keepdims=True) * (1.0 / D)
    m2 = jnp.sum(w * n, axis=1, keepdims=True) * (1.0 / D)
    return inv * (w - m1 - n * m2)


def ln2b_body(r0, c1, c3, h, c, keep, g, gh_ref, gp_ref, gg_ref, gb_ref, pb_ref):
    gn = r0[...] + c1[...].astype(f32) + c3[...].astype(f32)
    n, inv = stats(h[...])
    gh = c[...].astype(f32) + norm_back(gn * g[...], n, inv)
    gh_ref[...] = gh
    kg = keep[...] * gh
    gp_ref[...] = kg.astype(bf)
    acc_out(gg_ref, colsum(gn * n))
    acc_out(gb_ref, colsum(gn))
    acc_out(pb_ref, colsum(kg))


def ln2b_call(r0, c1, c3, h, c, keep, g):
    row = pl.BlockSpec((RB, D), lambda i: (i, 0))
    kp = pl.BlockSpec((RB, 1), lambda i: (i, 0))
    return pl.pallas_call(
        ln2b_body,
        grid=(TS // RB,),
        in_specs=[row, row, row, row, row, kp, full((1, D))],
        out_specs=[row, row] + [full((1, D))] * 3,
        out_shape=[sds((TS, D), f32), sds((TS, D), bf)] + [sds((1, D), f32)] * 3,
        compiler_params=params(),
        cost_estimate=cost(30 * TS * D, 20 * TS * D),
        name="ln2b",
    )(r0, c1, c3, h, c, keep, g)


def ln1b_body(r0, c1, c3, x, gh, keep, g, o_ref, gg_ref, gb_ref):
    gn = keep[...] * (r0[...] + c1[...].astype(f32) + c3[...].astype(f32))
    n, inv = stats(x[...].astype(f32))
    gt = (gh[...] + norm_back(gn * g[...], n, inv)).astype(bf)
    for k in range(NT):
        o_ref[k] = gt[:, k * TS : (k + 1) * TS]
    acc_out(gg_ref, colsum(gn * n))
    acc_out(gb_ref, colsum(gn))


def ln1b_call(r0, c1, c3, x, gh, keep, g):
    row = pl.BlockSpec((RB, D), lambda i: (i, 0))
    kp = pl.BlockSpec((RB, 1), lambda i: (i, 0))
    return pl.pallas_call(
        ln1b_body,
        grid=(TS // RB,),
        in_specs=[row, row, row, row, row, kp, full((1, D))],
        out_specs=[pl.BlockSpec((NT, RB, TS), lambda i: (0, i, 0))] + [full((1, D))] * 2,
        out_shape=[sds((NT, TS, TS), bf)] + [sds((1, D), f32)] * 2,
        compiler_params=params(),
        cost_estimate=cost(30 * TS * D, 18 * TS * D),
        name="ln1b",
    )(r0, c1, c3, x, gh, keep, g)


def pad_body(w_ref, q_ref, p_ref):
    rows = w_ref.shape[0]
    w = w_ref[...]
    zero = jnp.zeros((rows, HP - HDIM), bf)
    for h in range(3 * HL):
        q_ref[:, h * HP : (h + 1) * HP] = jnp.concatenate([w[:, h * HDIM : (h + 1) * HDIM], zero], axis=1)
    for h in range(HL):
        s = 3 * HL + h
        p_ref[:, h * HP : (h + 1) * HP] = jnp.concatenate([w[:, s * HDIM : (s + 1) * HDIM], zero], axis=1)


def pad_call(g1):
    rb = 160
    return pl.pallas_call(
        pad_body,
        grid=(D // rb,),
        in_specs=[pl.BlockSpec((rb, D), lambda i: (i, 0))],
        out_specs=[
            pl.BlockSpec((rb, 3 * HL * HP), lambda i: (i, 0)),
            pl.BlockSpec((rb, HL * HP), lambda i: (i, 0)),
        ],
        out_shape=[sds((D, 3 * HL * HP), bf), sds((D, HL * HP), bf)],
        compiler_params=params(),
        cost_estimate=cost(D * 2048, 2 * D * (1280 + 2048)),
        name="padw",
    )(g1)


def block_of(me, j):
    return lax.rem(me + j, NT)


def qkv_body(me_ref, x_ref, w_ref, b_ref, keep_ref, o_ref):
    o_ref[0] = (dot(x_ref[...], w_ref[...]) + b_ref[...]).astype(bf)


def qkv_call(me, j, x, w, bias, into):
    n = w.shape[1]
    tn = 256
    return pl.pallas_call(
        qkv_body,
        grid_spec=pltpu.PrefetchScalarGridSpec(
            num_scalar_prefetch=1,
            grid=(n // tn,),
            in_specs=[
                pl.BlockSpec((TS, D), lambda i, m: (0, 0)),
                pl.BlockSpec((D, tn), lambda i, m: (0, i)),
                pl.BlockSpec((1, tn), lambda i, m: (0, i)),
                ANY,
            ],
            out_specs=pl.BlockSpec((1, TS, tn), lambda i, m: (block_of(m[0], j), 0, i)),
        ),
        out_shape=sds((NT, TS, n), bf),
        input_output_aliases={4: 0},
        compiler_params=params(),
        cost_estimate=cost(2 * TS * D * n, 2 * (TS * D + D * n + TS * n)),
        name="qkv",
    )(me, x, w, bias, into)


def attn_body(qkv_ref, tab_ref, sel_ref, mask_ref, sp_ref, km_ref, z_ref, o_ref, p_ref, t_ref):
    @pl.when(pl.program_id(0) == 0)
    def _():
        t_ref[...] = dot(sel_ref[...], tab_ref[...]).astype(bf)

    table = t_ref[...]
    for h in range(HL):
        q = qkv_ref[:, h * HP : (h + 1) * HP]
        k = qkv_ref[:, (HL + h) * HP : (HL + h + 1) * HP]
        v = qkv_ref[:, (2 * HL + h) * HP : (2 * HL + h + 1) * HP]
        along = (dot_nt(q, table) * mask_ref[...].astype(f32)).astype(bf)
        s = dot_nt(q, k) * SCALE + dot(along, sp_ref[...]) + km_ref[...]
        top = jnp.max(s, axis=1, keepdims=True)
        e = jnp.exp(s - top)
        p = (e * (1.0 / jnp.sum(e, axis=1, keepdims=True))).astype(bf)
        p_ref[0, h] = p
        o_ref[:, h * HP : (h + 1) * HP] = dot(p, v).astype(bf)


def attn_call(qkv, tab, sel, mask, spread, keys, into):
    n = 3 * HL * HP
    return pl.pallas_call(
        attn_body,
        grid=(NW,),
        in_specs=[
            pl.BlockSpec((WR, n), lambda i: (i, 0)),
            full((64, HP)),
            full((512, 64)),
            full((WR, 512)),
            full((512, WR)),
            full((1, WR)),
            ANY,
        ],
        out_specs=[
            pl.BlockSpec((WR, HL * HP), lambda i: (i, 0)),
            pl.BlockSpec((1, HL, WR, WR), lambda i: (i, 0, 0, 0)),
        ],
        out_shape=[sds((NT * TS, HL * HP), bf), sds((NW, HL, WR, WR), bf)],
        scratch_shapes=[pltpu.VMEM((512, HP), bf)],
        input_output_aliases={6: 0},
        compiler_params=params(),
        cost_estimate=cost(24 * 6 * 2 * WR * WR * 256, 8e6, 24 * WR * 256),
        name="attn",
    )(qkv, tab, sel, mask, spread, keys, into)


def attnb_body(qkv_ref, p_ref, ga_ref, tab_ref, sel_ref, mask_ref, sp_ref, z_ref, o_ref, rel_ref, bias_ref, t_ref):
    @pl.when(pl.program_id(0) == 0)
    def _():
        t_ref[...] = dot(sel_ref[...], tab_ref[...]).astype(bf)
        rel_ref[...] = jnp.zeros_like(rel_ref)
        bias_ref[...] = jnp.zeros_like(bias_ref)

    table = t_ref[...]
    rel = jnp.zeros((512, HP), f32)
    for h in range(HL):
        cq = slice(h * HP, (h + 1) * HP)
        ck = slice((HL + h) * HP, (HL + h + 1) * HP)
        cv = slice((2 * HL + h) * HP, (2 * HL + h + 1) * HP)
        q = qkv_ref[:, cq]
        k = qkv_ref[:, ck]
        v = qkv_ref[:, cv]
        ga = ga_ref[:, cq]
        p = p_ref[0, h]
        pf = p.astype(f32)
        gs = dot_nt(ga, v)
        delta = jnp.sum(pf * gs, axis=1, keepdims=True)
        ds = (pf * (gs - delta)).astype(bf)
        gv = dot_tn(p, ga).astype(bf)
        gk = (dot_tn(ds, q) * SCALE).astype(bf)
        sums = (dot_nt(ds, sp_ref[...]) * mask_ref[...].astype(f32)).astype(bf)
        gq = (dot(ds, k) * SCALE + dot(sums, table)).astype(bf)
        rel = rel + dot_tn(sums, q)
        o_ref[:, cq] = gq
        o_ref[:, ck] = gk
        o_ref[:, cv] = gv
        bias_ref[:, cq] += colsum(gq.astype(f32))
        bias_ref[:, cv] += colsum(gv.astype(f32))
    rel_ref[...] += rel


def attnb_call(qkv, p, ga, tab, sel, mask, spread, into):
    n = 3 * HL * HP
    return pl.pallas_call(
        attnb_body,
        grid=(NW,),
        in_specs=[
            pl.BlockSpec((WR, n), lambda i: (i, 0)),
            pl.BlockSpec((1, HL, WR, WR), lambda i: (i, 0, 0, 0)),
            pl.BlockSpec((WR, HL * HP), lambda i: (i, 0)),
            full((64, HP)),
            full((512, 64)),
            full((WR, 512)),
            full((512, WR)),
            ANY,
        ],
        out_specs=[pl.BlockSpec((WR, n), lambda i: (i, 0)), full((512, HP)), full((1, n))],
        out_shape=[sds((NT * TS, n), bf), sds((512, HP), f32), sds((1, n), f32)],
        scratch_shapes=[pltpu.VMEM((512, HP), bf)],
        input_output_aliases={7: 0},
        compiler_params=params(),
        cost_estimate=cost(24 * 10 * 2 * WR * WR * 256, 14e6),
        name="attnb",
    )(qkv, p, ga, tab, sel, mask, spread, into)


def partial_body(me_ref, a_ref, w_ref, r0, r1, r2, r3):
    w = w_ref[...]
    for j, ref in ((2, r2), (1, r1), (3, r3), (0, r0)):
        ref[...] = dot_nt(a_ref[block_of(me_ref[0], j)], w).astype(ref.dtype)


def partial_call(me, a, w, name):
    k = a.shape[2]
    tn = 256
    return pl.pallas_call(
        partial_body,
        grid_spec=pltpu.PrefetchScalarGridSpec(
            num_scalar_prefetch=1,
            grid=(D // tn,),
            in_specs=[
                pl.BlockSpec((NT, TS, k), lambda i, m: (0, 0, 0)),
                pl.BlockSpec((tn, k), lambda i, m: (i, 0)),
            ],
            out_specs=[pl.BlockSpec((TS, tn), lambda i, m: (0, i))] * 4,
        ),
        out_shape=[sds((TS, D), f32)] + [sds((TS, D), bf)] * 3,
        compiler_params=params(),
        cost_estimate=cost(2 * NT * TS * D * k, 2 * (NT * TS * k + D * k + 5 * TS * D)),
        name=name,
    )(me, a, w)


def mlp_body(z_ref, gb_ref, w1_ref, w2_ref, b1_ref, act_ref, gp_ref, br_ref, gn_ref, fb_ref, br_s, gn_s):
    step = pl.program_id(0)
    w1 = w1_ref[...]
    w2 = w2_ref[...]
    pre = dot(z_ref[...], w1) + b1_ref[...]
    ga = dot(gb_ref[...], w2)
    cdf = 0.5 + 0.5 * lax.erf(pre * 0.7071067811865476)
    act = (pre * cdf).astype(bf)
    slope = cdf + pre * (0.3989422804014327 * jnp.exp(-0.5 * pre * pre))
    gp = (ga * slope).astype(bf)
    act_ref[...] = act
    gp_ref[...] = gp
    fb_ref[...] = colsum(gp.astype(f32))
    br = dot_nt(act, w2)
    gn = dot_nt(gp, w1)

    @pl.when(step == 0)
    def _():
        br_s[...] = br
        gn_s[...] = gn

    @pl.when(step > 0)
    def _():
        br_s[...] += br
        gn_s[...] += gn

    @pl.when(step == pl.num_programs(0) - 1)
    def _():
        br_ref[...] = br_s[...].astype(br_ref.dtype)
        gn_ref[...] = gn_s[...].astype(gn_ref.dtype)


def mlp_call(z, gb, w, b1, kind):
    tf = 256
    nf = D // tf
    col = pl.BlockSpec((TS, tf), lambda i: (0, i))
    return pl.pallas_call(
        mlp_body,
        grid=(nf,),
        in_specs=[
            full((TS, D)),
            full((TS, D)),
            pl.BlockSpec((D, tf), lambda i: (0, i)),
            pl.BlockSpec((D, tf), lambda i: (0, i + nf)),
            pl.BlockSpec((1, tf), lambda i: (0, i)),
        ],
        out_specs=[col, col, full((TS, D)), full((TS, D)), pl.BlockSpec((1, tf), lambda i: (0, i))],
        out_shape=[sds((TS, D), bf), sds((TS, D), bf), sds((TS, D), kind), sds((TS, D), kind), sds((1, D), f32)],
        scratch_shapes=[pltpu.VMEM((TS, D), f32), pltpu.VMEM((TS, D), f32)],
        compiler_params=params(),
        cost_estimate=cost(8 * TS * D * D, 4 * D * D + 12 * TS * D, 2 * TS * D),
        name="mlp",
    )(z, gb, w, w, b1)


def fcgrad_body(*refs):
    o_ref = refs[-1]
    z, gp, gb, act = refs[0:4], refs[4:8], refs[8:12], refs[12:16]
    total = dot_tn(z[0][...], gp[0][...])
    for j in range(1, NT):
        total += dot_tn(z[j][...], gp[j][...])
    o_ref[:, :D] = total.astype(bf)
    total = dot_tn(gb[0][...], act[0][...])
    for j in range(1, NT):
        total += dot_tn(gb[j][...], act[j][...])
    o_ref[:, D:] = total.astype(bf)


def fcgrad_call(z, gp, gb, act):
    td = 256
    col = pl.BlockSpec((TS, td), lambda i: (0, i))
    const = full((TS, D))
    return pl.pallas_call(
        fcgrad_body,
        grid=(D // td,),
        in_specs=[col] * 4 + [const] * 4 + [col] * 4 + [const] * 4,
        out_specs=pl.BlockSpec((td, 2 * D), lambda i: (i, 0)),
        out_shape=sds((D, 2 * D), bf),
        compiler_params=params(),
        cost_estimate=cost(16 * TS * D * D, 2 * (16 * TS * D + 2 * D * D)),
        name="fcgrad",
    )(*z, *gp, *gb, *act)


def narrow(x, heads):
    return jnp.concatenate([x[:, h * HP : h * HP + HDIM] for h in range(heads)], axis=1)


def qpgrad_body(me_ref, e0, e1, e2, e3, p0, p1, p2, p3, dq_ref, at_ref, o_ref):
    me = me_ref[0]
    total = None
    for j, e in enumerate((e0, e1, e2, e3)):
        part = dot_tn(e[...], dq_ref[block_of(me, j)])
        total = part if total is None else total + part
    o_ref[:, : 3 * HL * HDIM] = narrow(total, 3 * HL).astype(bf)
    total = None
    for j, p in enumerate((p0, p1, p2, p3)):
        part = dot_tn(p[...], at_ref[block_of(me, j)])
        total = part if total is None else total + part
    o_ref[:, 3 * HL * HDIM :] = narrow(total, HL).astype(bf)


def qpgrad_call(me, e, p, dqkv, att):
    td = 256
    col = pl.BlockSpec((TS, td), lambda i, m: (0, i))
    n = 3 * HL * HP
    return pl.pallas_call(
        qpgrad_body,
        grid_spec=pltpu.PrefetchScalarGridSpec(
            num_scalar_prefetch=1,
            grid=(D // td,),
            in_specs=[col] * 8
            + [
                pl.BlockSpec((NT, TS, n), lambda i, m: (0, 0, 0)),
                pl.BlockSpec((NT, TS, HL * HP), lambda i, m: (0, 0, 0)),
            ],
            out_specs=pl.BlockSpec((td, D), lambda i, m: (i, 0)),
        ),
        out_shape=sds((D, D), bf),
        compiler_params=params(),
        cost_estimate=cost(8 * TS * D * 2048, 2 * (8 * TS * D + 4 * TS * 2048 + D * D)),
        name="qpgrad",
    )(me, *e, *p, dqkv, att)


UP = [(i, (i + 1) % NT) for i in range(NT)]
DOWN = [(i, (i - 1) % NT) for i in range(NT)]


def up(v):
    return lax.ppermute(v, "tp", UP)


def down(v):
    return lax.ppermute(v, "tp", DOWN)


def ring_gather(own):
    b3 = up(own)
    b1 = down(own)
    b2 = jnp.concatenate([up(b3[:HALF]), down(b1[HALF:])], axis=0)
    return own, b1, b2, b3


def ring_scatter(r1, r2, r3):
    a = up(r2[:HALF])
    b = down(r2[HALF:])
    s1 = jnp.concatenate([(r1[:HALF].astype(f32) + a.astype(f32)).astype(bf), r1[HALF:]], axis=0)
    s3 = jnp.concatenate([r3[:HALF], (r3[HALF:].astype(f32) + b.astype(f32)).astype(bf)], axis=0)
    return down(s3), up(s1)


def from_everyone(array, axis):
    size = lax.axis_size(axis)
    return lax.all_to_all(jnp.broadcast_to(array[None], (size, *array.shape)), axis, 0, 0, tiled=True)


def windows(grid):
    n = grid.shape[-1]
    w = grid.reshape(2, WIN, 3, WIN, n).transpose(0, 2, 1, 3, 4).reshape(NW, CELLS, n)
    w = jnp.pad(w, ((0, 0), (0, WR - CELLS), (0, 0))).reshape(NW * WR, n)
    return jnp.pad(w, ((0, NT * TS - NW * WR), (0, 0))).reshape(NT, TS, n)


def unwindows(blocks):
    n = blocks.shape[-1]
    w = blocks.reshape(NT * TS, n)[: NW * WR].reshape(NW, WR, n)[:, :CELLS]
    return w.reshape(2, 3, WIN, WIN, n).transpose(0, 2, 1, 3, 4).reshape(2, WIN, 3 * WIN, n)


def local(
    tokens,
    valid_mask,
    ln1_gain,
    ln1_bias,
    qkv_weight,
    qkv_bias,
    rel_rows,
    rel_cols,
    proj_weight,
    proj_bias,
    ln2_gain,
    ln2_bias,
    fc1_weight,
    fc1_bias,
    fc2_weight,
    fc2_bias,
    cotangent,
):
    tp_index = lax.axis_index("tp")
    me = tp_index.astype(jnp.int32).reshape(1)
    sel, mask, spread, keys = rel_constants()
    sel = jnp.asarray(sel, bf)
    mask = jnp.asarray(mask, bf)
    spread = jnp.asarray(spread, bf)
    keys = jnp.asarray(keys, f32)
    row = lambda v: v.reshape(1, -1)

    own1 = jnp.concatenate([jnp.moveaxis(qkv_weight, 1, 0).reshape(80, 960), proj_weight.T], axis=1)
    own2 = jnp.concatenate([fc1_weight, fc2_weight.T], axis=1)
    all1 = lax.all_gather(own1, "shard", axis=0, tiled=True)
    all2 = lax.all_gather(own2, "shard", axis=0, tiled=True)
    qkvp, projp = pad_call(all1)
    bias_q = jnp.pad(qkv_bias.reshape(2, HL, HDIM), ((0, 0), (0, 0), (0, HP - HDIM))).reshape(2, HL * HP)
    bias_p = row(jnp.concatenate([bias_q[0], jnp.zeros((HL * HP,), f32), bias_q[1]]))
    tab = jnp.zeros((64, HP), bf).at[:RELS, :HDIM].set(rel_rows).at[32 : 32 + RELS, :HDIM].set(rel_cols)

    keep = windows(valid_mask.astype(f32)[..., None])
    keep = lax.dynamic_index_in_dim(keep, tp_index, 0, keepdims=False)
    tok4 = lax.all_to_all(windows(tokens), "tp", 0, 0, tiled=True)
    cot4 = lax.all_to_all(windows(cotangent), "tp", 0, 0, tiled=True)
    x, c, e, gb, sum_fc2_bias = ln1_call(tok4, cot4, keep, row(ln1_gain), row(ln1_bias))

    ents = ring_gather(e)
    qkv = jnp.zeros((NT, TS, 3 * HL * HP), bf)
    for j in (0, 1, 3, 2):
        qkv = qkv_call(me, j, ents[j], qkvp, bias_p, qkv)
    flat = qkv.reshape(NT * TS, 3 * HL * HP)
    att, probs = attn_call(flat, tab, sel, mask, spread, keys, jnp.zeros((NT * TS, HL * HP), bf))
    att4 = att.reshape(NT, TS, HL * HP)
    r0, r1, r2, r3 = partial_call(me, att4, projp, "proj")
    c1, c3 = ring_scatter(r1, r2, r3)
    h, z = ln2_call(r0, c1, c3, x, keep, row(proj_bias), row(ln2_gain), row(ln2_bias))

    gbs = ring_gather(gb)
    zs = ring_gather(z)
    mlp = {}
    for j in (0, 1, 3, 2):
        mlp[j] = mlp_call(zs[j], gbs[j], all2, row(fc1_bias), f32 if j == 0 else bf)
    acts = [mlp[j][0] for j in range(NT)]
    gpres = [mlp[j][1] for j in range(NT)]
    sum_fc1_bias = sum(mlp[j][4] for j in range(NT))
    c1, c3 = ring_scatter(mlp[1][3], mlp[2][3], mlp[3][3])
    grad2 = fcgrad_call(zs, gpres, gbs, acts)
    gh, gproj, sum_ln2_gain, sum_ln2_bias, sum_proj_bias = ln2b_call(
        mlp[0][3], c1, c3, h, c, keep, row(ln2_gain)
    )
    gps = ring_gather(gproj)
    own_fc = lax.psum_scatter(grad2, "shard", scatter_dimension=0, tiled=True)
    ga = jnp.zeros((NT, TS, HL * HP), bf)
    none = jnp.zeros((1, HL * HP), f32)
    for j in (0, 1, 3, 2):
        ga = qkv_call(me, j, gps[j], projp, none, ga)
    dqkv, rel, sum_qkv_bias = attnb_call(
        flat,
        probs,
        ga.reshape(NT * TS, HL * HP),
        tab,
        sel,
        mask,
        spread,
        jnp.zeros((NT * TS, 3 * HL * HP), bf),
    )
    dqkv4 = dqkv.reshape(NT, TS, 3 * HL * HP)
    r0, r1, r2, r3 = partial_call(me, dqkv4, qkvp, "gnorm1")
    c1, c3 = ring_scatter(r1, r2, r3)
    grad1 = qpgrad_call(me, ents, gps, dqkv4, att4)
    own_qp = lax.psum_scatter(grad1, "shard", scatter_dimension=0, tiled=True)
    gt4, sum_ln1_gain, sum_ln1_bias = ln1b_call(r0, c1, c3, x, gh, keep, row(ln1_gain))
    token_grads = unwindows(lax.all_to_all(gt4, "tp", 0, 0, tiled=True)).astype(f32)

    c1, c3 = ring_scatter(mlp[1][2], mlp[2][2], mlp[3][2])
    res4 = result_call(mlp[0][2], c1, c3, h, keep, row(fc2_bias))
    result = unwindows(lax.all_to_all(res4, "tp", 0, 0, tiled=True))

    rels = jnp.dot(sel.astype(f32).T, rel, precision=lax.Precision.HIGHEST)
    world = [
        sum_ln1_gain,
        sum_ln1_bias,
        sum_ln2_gain,
        sum_ln2_bias,
        sum_proj_bias,
        sum_fc2_bias,
        rels[:RELS, :HDIM],
        rels[32 : 32 + RELS, :HDIM],
    ]
    world = jnp.concatenate([v.ravel() for v in world])
    world = jnp.sum(from_everyone(world, "tp"), axis=0)
    qb = sum_qkv_bias.reshape(3, HL, HP)[:, :, :HDIM].reshape(3, HL * HDIM)
    every = jnp.concatenate([world, qb[0], qb[2], sum_fc1_bias.ravel()]).astype(bf)
    every = jnp.sum(from_everyone(every, ("shard", "ctx")).astype(f32), axis=0)
    cuts = [D] * 6 + [RELS * HDIM] * 2 + [2 * HL * HDIM, D]
    ends = np.cumsum([0] + cuts)
    small = [every[a:b] for a, b in zip(ends, ends[1:])]

    swap = [(0, 1), (1, 0)]
    fc = own_fc.astype(f32) + lax.ppermute(own_fc, "ctx", swap).astype(f32)
    qp = own_qp.astype(f32) + lax.ppermute(own_qp, "ctx", swap).astype(f32)
    return (
        result,
        token_grads,
        small[0],
        small[1],
        jnp.moveaxis(qp[:, :960].reshape(80, 3, 320), 0, 1),
        small[8].reshape(2, HL * HDIM),
        small[6].reshape(RELS, HDIM),
        small[7].reshape(RELS, HDIM),
        qp[:, 960:].T,
        small[4],
        small[2],
        small[3],
        fc[:, :D],
        small[9],
        fc[:, D:].T,
        small[5],
    )


def solution(mesh):
    cells = P("shard", "ctx", None, "tp")
    in_specs = (
        cells,
        P("shard", "ctx", None),
        P(),
        P(),
        P(None, "shard", "tp"),
        P(None, "tp"),
        P(),
        P(),
        P("tp", "shard"),
        P(),
        P(),
        P(),
        P("shard", "tp"),
        P("tp"),
        P("tp", "shard"),
        P(),
        cells,
    )
    out_specs = (
        cells,
        cells,
        P(),
        P(),
        P(None, "shard", "tp"),
        P(None, "tp"),
        P(),
        P(),
        P("tp", "shard"),
        P(),
        P(),
        P(),
        P("shard", "tp"),
        P("tp"),
        P("tp", "shard"),
        P(),
    )
    return jax.shard_map(local, mesh=mesh, in_specs=in_specs, out_specs=out_specs, check_vma=False)
```

time: 1330 us -> 578 us (0.43)
  the two profiles are of different devices: /device:TPU:0 before, /device:TPU:2 now
where the time goes in v1:
time: 578 us; the launch traced here: 567 us
  Pallas kernels  202 us (35%)
  waiting for transfers between devices  184 us (32%)
  starting transfers between devices  83.3 us (14%)
  local copies, waits for them, and re-layouts  57 us (10%)
  other arithmetic  16.4 us (3%)
  between operations  15.2 us (3%)
  blocking collectives  8.66 us (1%)
    ppermute x16, waiting for transfers between devices, up(): return lax.ppermute(v, 'tp', UP)  96.1 us
    pallas_call x4, Pallas kernels, mlp_call(): pl.pallas_call(mlp_body, grid=(nf,), in_specs=[full((TS, D)), full((TS, D...  45.3 us
    ppermute x16, starting transfers between devices, down(): return lax.ppermute(v, 'tp', DOWN)  43 us
    ppermute x16, waiting for transfers between devices, down(): return lax.ppermute(v, 'tp', DOWN)  42.2 us
    pallas_call x8, Pallas kernels, qkv_call(): pl.pallas_call(qkv_body, grid_spec=pltpu.PrefetchScalarGridSpec(num_scala...  36.5 us
    pallas_call x1, Pallas kernels, fcgrad_call(): pl.pallas_call(fcgrad_body, grid=(D // td,), in_specs=[col] * 4 + [const]...  19.5 us
    pallas_call x1, Pallas kernels, attnb_call(): pl.pallas_call(attnb_body, grid=(NW,), in_specs=[pl.BlockSpec((WR, n), la...  18.7 us
    pallas_call x1, Pallas kernels, qpgrad_call(): pl.pallas_call(qpgrad_body, grid_spec=pltpu.PrefetchScalarGridSpec(num_sc...  16.7 us
  transfers between devices with their start and end apart: 43, of which 24 were waited for; matrix products, arithmetic and copies ran while one was open for 10% of the time, Pallas kernels for 26%

profile of v1, /device:TPU:2, one launch (start us, length us, event | category | flops | bytes accessed | tf_op | source)
XLA Modules:
  0.0 567.0 jit_solution(7174173353594396690)
XLA Ops:
  13.8 4.8 all-to-all-start
  20.6 11.0 %all-to-all-done.tok_ref = bf16[4,320,320]{2,1,0:T(8,128)(2,1)S(1)} async-done(((bf16[4,320,320]{2,1,0:T(8,128)(2,1)}), bf16[4,320,320]{2,1,0:T(8,128)(2,1)S(1)}, u32[]{:S(2)}, u32[]{:S(2)}) %all-to-all-start) | async-done | bytes 819232 | tf_op jit(solution)/shard_map/all_to_all | solution.py:639
  31.6 4.9 all-to-all-start.1
  39.0 9.5 %all-to-all-done.1.cot_ref = bf16[4,320,320]{2,1,0:T(8,128)(2,1)S(1)} async-done(((bf16[4,320,320]{2,1,0:T(8,128)(2,1)}), bf16[4,320,320]{2,1,0:T(8,128)(2,1)S(1)}, u32[]{:S(2)}, u32[]{:S(2)}) %all-to-all-start.1) | async-done | bytes 819232 | tf_op jit(solution)/shard_map/all_to_all | solution.py:640
  49.6 4.8 ln1.1
  56.5 16.1 %collective-permute-done.x_ref.e3 = bf16[320,1280]{1,0:T(8,128)(2,1)S(1)} collective-permute-done((bf16[320,1280]{1,0:T(8,128)(2,1)}, bf16[320,1280]{1,0:T(8,128)(2,1)S(1)}, u32[]{:S(2)}, u32[]{:S(2)}) %collective-permute-start) | collective-permute-done | bytes 819232 | tf_op jit(solution)/shard_map/ppermute | solution.py:560
  77.4 4.4 collective-permute-done.1
  82.4 7.7 %padw.1 = (bf16[1280,1536]{1,0:T(8,128)(2,1)}, bf16[1280,512]{1,0:T(8,128)(2,1)}) custom-call(bf16[1280,1280]{1,0:T(8,128)(2,1)} %all-gather.3.cloned.1.call-done.w_ref), custom_call_target="tpu_custom_call" | custom-call | flops 2621440 | bytes 8519680 | tf_op jit(solution)/shard_map/padw/pallas_call | solution.py:250
  92.3 6.3 %qkv.8.keep_ref = bf16[4,320,1536]{2,1,0:T(8,128)(2,1)} custom-call(s32[1]{0:T(128)} %bitcast.me_ref, bf16[320,1280]{1,0:T(8,128)(2,1)} %get-tuple-element.90.x_ref.e0, bf16[1280,1536]{1,0:T(8,128)(2,1)} %get-tuple-element.91.w_ref, f32[1,1536]{1,0:T(1,128)} %reshape.329.b_ref, ...), custom_call_target="tpu_custom_call", output_to_operand_aliasing={{}: (4, {})} | custom-call | flops 1258291200 | bytes 5734400 | tf_op jit(solution)/shard_map/qkv/pallas_call | solution.py:276
  98.6 6.3 %qkv.9.keep_ref = bf16[4,320,1536]{2,1,0:T(8,128)(2,1)} custom-call(s32[1]{0:T(128)} %bitcast.me_ref, bf16[320,1280]{1,0:T(8,128)(2,1)} %copy-done.3, bf16[1280,1536]{1,0:T(8,128)(2,1)} %get-tuple-element.91.w_ref, f32[1,1536]{1,0:T(1,128)} %reshape.329.b_ref, bf16[4,320,1536]{2,1,0:T(8,128)(2,1)} %qkv.8.keep_ref), custom_call_target="tpu_custom_call", output_to_operand_aliasing={{}: (4, {})} | custom-call | flops 1258291200 | bytes 5734400 | tf_op jit(solution)/shard_map/qkv/pallas_call | solution.py:276
  104.9 6.3 %qkv.10.keep_ref = bf16[4,320,1536]{2,1,0:T(8,128)(2,1)} custom-call(s32[1]{0:T(128)} %bitcast.me_ref, bf16[320,1280]{1,0:T(8,128)(2,1)} %copy-done.2, bf16[1280,1536]{1,0:T(8,128)(2,1)} %get-tuple-element.91.w_ref, f32[1,1536]{1,0:T(1,128)} %reshape.329.b_ref, bf16[4,320,1536]{2,1,0:T(8,128)(2,1)} %qkv.9.keep_ref), custom_call_target="tpu_custom_call", output_to_operand_aliasing={{}: (4, {})} | custom-call | flops 1258291200 | bytes 5734400 | tf_op jit(solution)/shard_map/qkv/pallas_call | solution.py:276
  111.1 6.3 %qkv.11 = bf16[4,320,1536]{2,1,0:T(8,128)(2,1)} custom-call(s32[1]{0:T(128)} %bitcast.me_ref, bf16[320,1280]{1,0:T(8,128)(2,1)} %copy-done.6, bf16[1280,1536]{1,0:T(8,128)(2,1)} %get-tuple-element.91.w_ref, f32[1,1536]{1,0:T(1,128)} %reshape.329.b_ref, bf16[4,320,1536]{2,1,0:T(8,128)(2,1)} %qkv.10.keep_ref), custom_call_target="tpu_custom_call", output_to_operand_aliasing={{}: (4, {})} | custom-call | flops 1258291200 | bytes 5734400 | tf_op jit(solution)/shard_map/qkv/pallas_call | solution.py:276
  118.6 16.7 %attn.1 = (bf16[1280,512]{1,0:T(8,128)(2,1)}, bf16[6,4,208,208]{3,2,1,0:T(8,128)(2,1)}) custom-call(bf16[1280,1536]{1,0:T(8,128)(2,1)} %bitcast.46, bf16[64,128]{1,0:T(8,128)(2,1)} %copy-done.33, bf16[512,64]{1,0:T(8,128)(2,1)} %constant.84.clone.sel_ref, bf16[208,512]{1,0:T(8,128)(2,1)} %constant.85.clone.mask_ref, ...), custom_call_target="tpu_custom_call", output_to_operand_aliasing={{0}: (6, {})} | custom-call | flops 3189768192 | bytes 8000000 | tf_op jit(solution)/shard_map/attn/pallas_call | solution.py:318
  135.3 6.1 %proj.1 = (f32[320,1280]{1,0:T(8,128)}, bf16[320,1280]{1,0:T(8,128)(2,1)}, bf16[320,1280]{1,0:T(8,128)(2,1)}, bf16[320,1280]{1,0:T(8,128)(2,1)}) custom-call(s32[1]{0:T(128)} %bitcast.me_ref, bf16[4,320,512]{2,1,0:T(8,128)(2,1)} %bitcast.62, bf16[1280,512]{1,0:T(8,128)(2,1)} %get-tuple-element.93.w_ref), custom_call_target="tpu_custom_call" | custom-call | flops 1677721600 | bytes 6717440 | tf_op jit(solution)/shard_map/proj/pallas_call | solution.py:412
  146.0 6.9 %collective-permute-done.4 = bf16[160,1280]{1,0:T(8,128)(2,1)S(1)} collective-permute-done((bf16[160,1280]{1,0:T(8,128)(2,1)S(1)}, bf16[160,1280]{1,0:T(8,128)(2,1)S(1)}, u32[]{:S(2)}, u32[]{:S(2)}) %collective-permute-start.4) | collective-permute-done | bytes 409632 | tf_op jit(solution)/shard_map/ppermute | solution.py:564
  162.8 12.6 %collective-permute-done.5.c1 = bf16[320,1280]{1,0:T(8,128)(2,1)S(1)} collective-permute-done((bf16[320,1280]{1,0:T(8,128)(2,1)S(1)}, bf16[320,1280]{1,0:T(8,128)(2,1)S(1)}, u32[]{:S(2)}, u32[]{:S(2)}) %collective-permute-start.5) | collective-permute-done | bytes 819232 | tf_op jit(solution)/shard_map/ppermute | solution.py:564
  175.4 4.4 collective-permute-done.7.c3
  180.8 4.6 ln2.1
  188.8 8.6 %collective-permute-done.9.gb_ref.refs_11_ = bf16[320,1280]{1,0:T(8,128)(2,1)S(1)} collective-permute-done((bf16[320,1280]{1,0:T(8,128)(2,1)}, bf16[320,1280]{1,0:T(8,128)(2,1)S(1)}, u32[]{:S(2)}, u32[]{:S(2)}) %collective-permute-start.9) | collective-permute-done | bytes 819232 | tf_op jit(solution)/shard_map/ppermute | solution.py:560
  201.5 13.5 %collective-permute-done.8.z_ref.refs_3_ = bf16[320,1280]{1,0:T(8,128)(2,1)S(1)} collective-permute-done((bf16[320,1280]{1,0:T(8,128)(2,1)}, bf16[320,1280]{1,0:T(8,128)(2,1)S(1)}, u32[]{:S(2)}, u32[]{:S(2)}) %collective-permute-start.8) | collective-permute-done | bytes 819232 | tf_op jit(solution)/shard_map/ppermute | solution.py:560
  215.1 6.1 %collective-permute-done.13 = bf16[160,1280]{1,0:T(8,128)(2,1)S(1)} collective-permute-done((bf16[160,1280]{1,0:T(8,128)(2,1)S(1)}, bf16[160,1280]{1,0:T(8,128)(2,1)S(1)}, u32[]{:S(2)}, u32[]{:S(2)}) %collective-permute-start.13) | collective-permute-done | bytes 409632 | tf_op jit(solution)/shard_map/ppermute | solution.py:560
  225.6 4.5 collective-permute-done.12
  231.0 11.1 %mlp.6 = (bf16[320,1280]{1,0:T(8,128)(2,1)}, bf16[320,1280]{1,0:T(8,128)(2,1)}, bf16[320,1280]{1,0:T(8,128)(2,1)}, bf16[320,1280]{1,0:T(8,128)(2,1)}, f32[1,1280]{1,0:T(1,128)}) custom-call(bf16[320,1280]{1,0:T(8,128)(2,1)} %copy-done.31, bf16[320,1280]{1,0:T(8,128)(2,1)} %copy-done.30, bf16[1280,2560]{1,0:T(8,128)(2,1)} %all-gather.5.cloned.1.call-done.w1_ref.w2_ref, ...), custom_call_target="tpu_custom_call" | custom-call | flops 4194304000 | bytes 11468800 | tf_op jit(solution)/shard_map/mlp/pallas_call | solution.py:466
  245.9 11.1 %mlp.5 = (bf16[320,1280]{1,0:T(8,128)(2,1)}, bf16[320,1280]{1,0:T(8,128)(2,1)}, bf16[320,1280]{1,0:T(8,128)(2,1)}, bf16[320,1280]{1,0:T(8,128)(2,1)}, f32[1,1280]{1,0:T(1,128)}) custom-call(bf16[320,1280]{1,0:T(8,128)(2,1)} %copy-done.28, bf16[320,1280]{1,0:T(8,128)(2,1)} %copy-done.26, bf16[1280,2560]{1,0:T(8,128)(2,1)} %all-gather.5.cloned.1.call-done.w1_ref.w2_ref, ...), custom_call_target="tpu_custom_call" | custom-call | flops 4194304000 | bytes 11468800 | tf_op jit(solution)/shard_map/mlp/pallas_call | solution.py:466
  258.1 11.2 %mlp.7 = (bf16[320,1280]{1,0:T(8,128)(2,1)}, bf16[320,1280]{1,0:T(8,128)(2,1)}, bf16[320,1280]{1,0:T(8,128)(2,1)}, bf16[320,1280]{1,0:T(8,128)(2,1)}, f32[1,1280]{1,0:T(1,128)}) custom-call(bf16[320,1280]{1,0:T(8,128)(2,1)} %copy-done.29, bf16[320,1280]{1,0:T(8,128)(2,1)} %copy-done.27, bf16[1280,2560]{1,0:T(8,128)(2,1)} %all-gather.5.cloned.1.call-done.w1_ref.w2_ref, ...), custom_call_target="tpu_custom_call" | custom-call | flops 4194304000 | bytes 11468800 | tf_op jit(solution)/shard_map/mlp/pallas_call | solution.py:466
  272.7 10.1 %collective-permute-done.22 = bf16[160,1280]{1,0:T(8,128)(2,1)S(1)} collective-permute-done((bf16[160,1280]{1,0:T(8,128)(2,1)S(1)}, bf16[160,1280]{1,0:T(8,128)(2,1)S(1)}, u32[]{:S(2)}, u32[]{:S(2)}) %collective-permute-start.22) | collective-permute-done | bytes 409632 | tf_op jit(solution)/shard_map/ppermute | solution.py:560
  283.3 11.8 %mlp.4 = (bf16[320,1280]{1,0:T(8,128)(2,1)}, bf16[320,1280]{1,0:T(8,128)(2,1)}, f32[320,1280]{1,0:T(8,128)}, f32[320,1280]{1,0:T(8,128)}, f32[1,1280]{1,0:T(1,128)}) custom-call(bf16[320,1280]{1,0:T(8,128)(2,1)} %get-tuple-element.99.z_ref.refs_0_, bf16[320,1280]{1,0:T(8,128)(2,1)} %get-tuple-element.100.gb_ref.refs_8_, ...), custom_call_target="tpu_custom_call" | custom-call | flops 4194304000 | bytes 11468800 | tf_op jit(solution)/shard_map/mlp/pallas_call | solution.py:466
  298.3 5.7 ln2b.1
  307.6 14.4 %collective-permute-done.24.x_ref.p3 = bf16[320,1280]{1,0:T(8,128)(2,1)S(1)} collective-permute-done((bf16[320,1280]{1,0:T(8,128)(2,1)}, bf16[320,1280]{1,0:T(8,128)(2,1)S(1)}, u32[]{:S(2)}, u32[]{:S(2)}) %collective-permute-start.24) | collective-permute-done | bytes 819232 | tf_op jit(solution)/shard_map/ppermute | solution.py:560
  341.5 18.7 %attnb.1 = (bf16[1280,1536]{1,0:T(8,128)(2,1)}, f32[512,128]{1,0:T(8,128)}, f32[1,1536]{1,0:T(1,128)}) custom-call(bf16[1280,1536]{1,0:T(8,128)(2,1)} %bitcast.47, bf16[6,4,208,208]{3,2,1,0:T(8,128)(2,1)} %get-tuple-element.106.p_ref, bf16[1280,512]{1,0:T(8,128)(2,1)} %bitcast.48, bf16[64,128]{1,0:T(8,128)(2,1)} %copy-done.33, ...), custom_call_target="tpu_custom_call", output_to_operand_aliasing={{0}: (7, {})} | custom-call | flops 5316280320 | bytes 14000000 | tf_op jit(solution)/shard_map/attnb/pallas_call | solution.py:380
  360.2 16.7 %qpgrad.1 = bf16[1280,1280]{1,0:T(8,128)(2,1)} custom-call(s32[1]{0:T(128)} %bitcast.me_ref, bf16[320,1280]{1,0:T(8,128)(2,1)} %get-tuple-element.90.x_ref.e0, bf16[320,1280]{1,0:T(8,128)(2,1)} %copy-done.3, bf16[320,1280]{1,0:T(8,128)(2,1)} %copy-done.6, bf16[320,1280]{1,0:T(8,128)(2,1)} %copy-done.2, bf16[320,1280]{1,0:T(8,128)(2,1)} %get-tuple-element.112.x_ref.p0, ...), custom_call_target="tpu_custom_call" | custom-call | flops 6710886400 | bytes 15073280 | tf_op jit(solution)/shard_map/qpgrad/pallas_call | solution.py:536
  377.1 19.5 %fcgrad.1 = bf16[1280,2560]{1,0:T(8,128)(2,1)} custom-call(bf16[320,1280]{1,0:T(8,128)(2,1)} %get-tuple-element.99.z_ref.refs_0_, bf16[320,1280]{1,0:T(8,128)(2,1)} %copy-done.29, bf16[320,1280]{1,0:T(8,128)(2,1)} %copy-done.31, bf16[320,1280]{1,0:T(8,128)(2,1)} %copy-done.28, bf16[320,1280]{1,0:T(8,128)(2,1)} %get-tuple-element.132.refs_4_, ...), custom_call_target="tpu_custom_call" | custom-call | flops 8388608000 | bytes 19660800 | tf_op jit(solution)/shard_map/fcgrad/pallas_call | solution.py:502
  401.6 7.8 %collective-permute-done.16 = bf16[160,1280]{1,0:T(8,128)(2,1)S(1)} collective-permute-done((bf16[160,1280]{1,0:T(8,128)(2,1)S(1)}, bf16[160,1280]{1,0:T(8,128)(2,1)S(1)}, u32[]{:S(2)}, u32[]{:S(2)}) %collective-permute-start.16) | collective-permute-done | bytes 409632 | tf_op jit(solution)/shard_map/ppermute | solution.py:564
  412.1 9.5 %gnorm1.1 = (f32[320,1280]{1,0:T(8,128)}, bf16[320,1280]{1,0:T(8,128)(2,1)}, bf16[320,1280]{1,0:T(8,128)(2,1)}, bf16[320,1280]{1,0:T(8,128)(2,1)}) custom-call(s32[1]{0:T(128)} %bitcast.me_ref, bf16[4,320,1536]{2,1,0:T(8,128)(2,1)} %bitcast.54, bf16[1280,1536]{1,0:T(8,128)(2,1)} %get-tuple-element.91.w_ref), custom_call_target="tpu_custom_call" | custom-call | flops 5033164800 | bytes 11960320 | tf_op jit(solution)/shard_map/gnorm1/pallas_call | solution.py:412
  425.3 9.8 %collective-permute-done.28 = bf16[160,1280]{1,0:T(8,128)(2,1)S(1)} collective-permute-done((bf16[160,1280]{1,0:T(8,128)(2,1)S(1)}, bf16[160,1280]{1,0:T(8,128)(2,1)S(1)}, u32[]{:S(2)}, u32[]{:S(2)}) %collective-permute-start.28) | collective-permute-done | bytes 409632 | tf_op jit(solution)/shard_map/ppermute | solution.py:564
  437.8 15.1 %collective-permute-done.30 = bf16[160,1280]{1,0:T(8,128)(2,1)S(1)} collective-permute-done((bf16[160,1280]{1,0:T(8,128)(2,1)S(1)}, bf16[160,1280]{1,0:T(8,128)(2,1)S(1)}, u32[]{:S(2)}, u32[]{:S(2)}) %collective-permute-start.30) | collective-permute-done | bytes 409632 | tf_op jit(solution)/shard_map/ppermute | solution.py:560
  455.0 4.6 result.1
  459.7 6.8 %all-to-all-start.2 = ((bf16[4,320,320]{2,1,0:T(8,128)(2,1)}), bf16[4,320,320]{2,1,0:T(8,128)(2,1)S(1)}, u32[]{:S(2)}, u32[]{:S(2)}) async-start(bf16[4,320,320]{2,1,0:T(8,128)(2,1)} %result.1), calls=%async_computation.2 | async-start | bytes 1966080 | tf_op jit(solution)/shard_map/all_to_all | solution.py:693
  467.2 5.5 ln1b.1
  474.2 6.2 %all-to-all-done.2 = bf16[4,320,320]{2,1,0:T(8,128)(2,1)S(1)} async-done(((bf16[4,320,320]{2,1,0:T(8,128)(2,1)}), bf16[4,320,320]{2,1,0:T(8,128)(2,1)S(1)}, u32[]{:S(2)}, u32[]{:S(2)}) %all-to-all-start.2) | async-done | bytes 819232 | tf_op jit(solution)/shard_map/all_to_all | solution.py:693
  480.5 8.7 %all_to_all.32 = f32[4,1,12000]{2,1,0:T(1,128)S(1)} all-to-all(f32[4,1,12000]{2,1,0:T(1,128)S(1)} %broadcast_in_dim.37), channel_id=1, replica_groups=mesh['shard'=16,'ctx'=2,'tp'=4] {'tp'}, dimensions={0} | all-to-all | bytes 384000 | tf_op jit(solution)/shard_map/all_to_all | solution.py:584
  489.1 5.8 %all-to-all-start.3 = ((bf16[4,320,320]{2,1,0:T(8,128)(2,1)}), bf16[4,320,320]{2,1,0:T(8,128)(2,1)}, u32[]{:S(2)}, u32[]{:S(2)}) async-start(bf16[4,320,320]{2,1,0:T(8,128)(2,1)} %get-tuple-element.119), calls=%async_computation.3 | async-start | bytes 1966080 | tf_op jit(solution)/shard_map/all_to_all | solution.py:689
  497.0 7.2 %reduce.20 = bf16[32,13920]{1,0:T(8,128)(2,1)} reduce(bf16[32,1,13920]{2,1,0:T(2,128)(2,1)S(1)} %broadcast_in_dim.38, bf16[]{:T(256)} %broadcast.71), dimensions={1}, to_apply=%broadcast_in_dim.38.reduce_sub_computation | reduce | bytes 1781762 | tf_op jit(solution)/shard_map/broadcast_in_dim | solution.py:584
  507.6 8.2 %all-to-all-start.5 = ((bf16[32,2,6960]{2,1,0:T(2,128)(2,1)}), bf16[32,2,6960]{2,1,0:T(2,128)(2,1)}, u32[]{:S(2)}, u32[]{:S(2)}) async-start(bf16[32,2,6960]{2,1,0:T(2,128)(2,1)} %reshape.372), calls=%async_computation.5 | async-start | bytes 1802240 | tf_op jit(solution)/shard_map/all_to_all | solution.py:584
  525.0 9.2 %all-to-all-done.5 = bf16[32,2,6960]{2,1,0:T(2,128)(2,1)} async-done(((bf16[32,2,6960]{2,1,0:T(2,128)(2,1)}), bf16[32,2,6960]{2,1,0:T(2,128)(2,1)}, u32[]{:S(2)}, u32[]{:S(2)}) %all-to-all-start.5) | async-done | bytes 890912 | tf_op jit(solution)/shard_map/all_to_all | solution.py:584
  534.2 5.5 reshape.373
  546.3 5.4 collective-permute-done.32
  554.4 4.8 collective-permute-done.33
  (307 shorter events, 129.2 us)
Async XLA Ops:
  7.2 75.2 %all-gather.3.cloned.1.call-start = ((), (), s32[]{:S(2)}) async-start(), calls=%async_computation.8 | async-start | bytes 3481600 | tf_op jit(solution)/shard_map/all_gather | solution.py:630
  10.1 220.0 %all-gather.5.cloned.1.call-start = ((), (), s32[]{:S(2)}) async-start(), calls=%async_computation.9 | async-start | bytes 6963200 | tf_op jit(solution)/shard_map/all_gather | solution.py:631
  13.8 17.8 %all-to-all-start = ((bf16[4,320,320]{2,1,0:T(8,128)(2,1)}), bf16[4,320,320]{2,1,0:T(8,128)(2,1)S(1)}, u32[]{:S(2)}, u32[]{:S(2)}) async-start(bf16[4,320,320]{2,1,0:T(8,128)(2,1)} %bitcast.4), calls=%async_computation | async-start | bytes 1966080 | tf_op jit(solution)/shard_map/all_to_all | solution.py:639
  31.6 17.0 %all-to-all-start.1 = ((bf16[4,320,320]{2,1,0:T(8,128)(2,1)}), bf16[4,320,320]{2,1,0:T(8,128)(2,1)S(1)}, u32[]{:S(2)}, u32[]{:S(2)}) async-start(bf16[4,320,320]{2,1,0:T(8,128)(2,1)} %bitcast.8), calls=%async_computation.1 | async-start | bytes 1966080 | tf_op jit(solution)/shard_map/all_to_all | solution.py:640
  36.5 505.5 %reduce-scatter.3.cloned.1.call-start = ((), (), s32[]{:S(2)}) async-start(), calls=%async_computation.10 | async-start | bytes 3481600 | tf_op jit(solution)/shard_map/reduce_scatter | solution.py:687
  36.7 36.3 %copy-start.53 = (f32[2,320]{1,0:T(2,128)S(1)}, f32[2,320]{1,0:T(2,128)}, u32[]{:S(2)}) copy-start(f32[2,320]{1,0:T(2,128)} %param.30) | copy-start | bytes 7684
  39.0 37.9 %copy-start.35 = (bf16[27,80]{1,0:T(8,128)(2,1)S(1)}, bf16[27,80]{1,0:T(8,128)(2,1)}, u32[]{:S(2)}) copy-start(bf16[27,80]{1,0:T(8,128)(2,1)} %param.31) | copy-start | bytes 12964
  39.0 37.9 %copy-start.36 = (bf16[27,80]{1,0:T(8,128)(2,1)S(1)}, bf16[27,80]{1,0:T(8,128)(2,1)}, u32[]{:S(2)}) copy-start(bf16[27,80]{1,0:T(8,128)(2,1)} %param.32) | copy-start | bytes 12964
  54.4 18.1 %collective-permute-start = (bf16[320,1280]{1,0:T(8,128)(2,1)}, bf16[320,1280]{1,0:T(8,128)(2,1)S(1)}, u32[]{:S(2)}, u32[]{:S(2)}) collective-permute-start(bf16[320,1280]{1,0:T(8,128)(2,1)} %get-tuple-element.90.x_ref.e0), channel_id=1, source_target_pairs={{0,1},{1,2},{2,3},{3,0},{4,5},{5,6},{6,7},{7,4},{8,9},{9,10},{10,1... | collective-permute-start | bytes 2457608 | tf_op jit(solution)/shard_map/ppermute | solution.py:560
  54.5 18.6 %collective-permute-start.2 = (bf16[320,1280]{1,0:T(8,128)(2,1)}, bf16[320,1280]{1,0:T(8,128)(2,1)S(1)}, u32[]{:S(2)}, u32[]{:S(2)}) collective-permute-start(bf16[320,1280]{1,0:T(8,128)(2,1)} %get-tuple-element.90.x_ref.e0), channel_id=1, source_target_pairs={{0,3},{1,0},{2,1},{3,2},{4,7},{5,4},{6,5},{7,6},{8,11},{9,8},{10,9... | collective-permute-start | bytes 2457608 | tf_op jit(solution)/shard_map/ppermute | solution.py:564
  72.6 9.2 %collective-permute-start.1 = (bf16[160,1280]{1,0:T(8,128)(2,1)S(1)}, bf16[160,1280]{1,0:T(8,128)(2,1)S(1)}, u32[]{:S(2)}, u32[]{:S(2)}) collective-permute-start(bf16[160,1280]{1,0:T(8,128)(2,1)S(1)} %slice.292), channel_id=1, source_target_pairs={{0,1},{1,2},{2,3},{3,0},{4,5},{5,6},{6,7},{7,4},{8,9},{9,10},{10,1... | collective-permute-start | bytes 1228808 | tf_op jit(solution)/shard_map/ppermute | solution.py:560
  73.9 8.4 %collective-permute-start.3 = (bf16[160,1280]{1,0:T(8,128)(2,1)}, bf16[160,1280]{1,0:T(8,128)(2,1)S(1)}, u32[]{:S(2)}, u32[]{:S(2)}) collective-permute-start(bf16[160,1280]{1,0:T(8,128)(2,1)} %slice.293), channel_id=1, source_target_pairs={{0,3},{1,0},{2,1},{3,2},{4,7},{5,4},{6,5},{7,6},{8,11},{9,8},{10,9... | collective-permute-start | bytes 1228808 | tf_op jit(solution)/shard_map/ppermute | solution.py:564
  142.7 10.2 %collective-permute-start.4 = (bf16[160,1280]{1,0:T(8,128)(2,1)S(1)}, bf16[160,1280]{1,0:T(8,128)(2,1)S(1)}, u32[]{:S(2)}, u32[]{:S(2)}) collective-permute-start(bf16[160,1280]{1,0:T(8,128)(2,1)S(1)} %get-tuple-element.229), channel_id=1, source_target_pairs={{0,3},{1,0},{2,1},{3,2},{4,7},{5,4},{6,5},{7,6},{8,11},{9,8},{10,9... | collective-permute-start | bytes 1228808 | tf_op jit(solution)/shard_map/ppermute | solution.py:564
  145.8 11.1 %collective-permute-start.6 = (bf16[160,1280]{1,0:T(8,128)(2,1)S(1)}, bf16[160,1280]{1,0:T(8,128)(2,1)S(1)}, u32[]{:S(2)}, u32[]{:S(2)}) collective-permute-start(bf16[160,1280]{1,0:T(8,128)(2,1)S(1)} %get-tuple-element.228), channel_id=1, source_target_pairs={{0,1},{1,2},{2,3},{3,0},{4,5},{5,6},{6,7},{7,4},{8,9},{9,10},{10,1... | collective-permute-start | bytes 1228808 | tf_op jit(solution)/shard_map/ppermute | solution.py:560
  153.1 22.3 %collective-permute-start.5 = (bf16[320,1280]{1,0:T(8,128)(2,1)S(1)}, bf16[320,1280]{1,0:T(8,128)(2,1)S(1)}, u32[]{:S(2)}, u32[]{:S(2)}) collective-permute-start(bf16[320,1280]{1,0:T(8,128)(2,1)S(1)} %pad_maximum_fusion), channel_id=1, source_target_pairs={{0,3},{1,0},{2,1},{3,2},{4,7},{5,4},{6,5},{7,6},{8,11},{9,8},{10,9... | collective-permute-start | bytes 2457608 | tf_op jit(solution)/shard_map/ppermute | solution.py:564
  157.1 22.7 %collective-permute-start.7 = (bf16[320,1280]{1,0:T(8,128)(2,1)S(1)}, bf16[320,1280]{1,0:T(8,128)(2,1)S(1)}, u32[]{:S(2)}, u32[]{:S(2)}) collective-permute-start(bf16[320,1280]{1,0:T(8,128)(2,1)S(1)} %pad_maximum_fusion.1), channel_id=1, source_target_pairs={{0,1},{1,2},{2,3},{3,0},{4,5},{5,6},{6,7},{7,4},{8,9},{9,10},{10,1... | collective-permute-start | bytes 2457608 | tf_op jit(solution)/shard_map/ppermute | solution.py:560
  157.2 40.2 %collective-permute-start.9 = (bf16[320,1280]{1,0:T(8,128)(2,1)}, bf16[320,1280]{1,0:T(8,128)(2,1)S(1)}, u32[]{:S(2)}, u32[]{:S(2)}) collective-permute-start(bf16[320,1280]{1,0:T(8,128)(2,1)} %get-tuple-element.100.gb_ref.refs_8_), channel_id=1, source_target_pairs={{0,1},{1,2},{2,3},{3,0},{4,5},{5,6},{6,7},{7,4},{8,9},{9,10},{10,1... | collective-permute-start | bytes 2457608 | tf_op jit(solution)/shard_map/ppermute | solution.py:560
  160.0 37.5 %collective-permute-start.14 = (bf16[320,1280]{1,0:T(8,128)(2,1)}, bf16[320,1280]{1,0:T(8,128)(2,1)S(1)}, u32[]{:S(2)}, u32[]{:S(2)}) collective-permute-start(bf16[320,1280]{1,0:T(8,128)(2,1)} %get-tuple-element.100.gb_ref.refs_8_), channel_id=1, source_target_pairs={{0,3},{1,0},{2,1},{3,2},{4,7},{5,4},{6,5},{7,6},{8,11},{9,8},{10,9... | collective-permute-start | bytes 2457608 | tf_op jit(solution)/shard_map/ppermute | solution.py:564
  185.4 29.5 %collective-permute-start.8 = (bf16[320,1280]{1,0:T(8,128)(2,1)}, bf16[320,1280]{1,0:T(8,128)(2,1)S(1)}, u32[]{:S(2)}, u32[]{:S(2)}) collective-permute-start(bf16[320,1280]{1,0:T(8,128)(2,1)} %get-tuple-element.99.z_ref.refs_0_), channel_id=1, source_target_pairs={{0,1},{1,2},{2,3},{3,0},{4,5},{5,6},{6,7},{7,4},{8,9},{9,10},{10,1... | collective-permute-start | bytes 2457608 | tf_op jit(solution)/shard_map/ppermute | solution.py:560
  185.5 35.7 %collective-permute-start.11 = (bf16[320,1280]{1,0:T(8,128)(2,1)}, bf16[320,1280]{1,0:T(8,128)(2,1)S(1)}, u32[]{:S(2)}, u32[]{:S(2)}) collective-permute-start(bf16[320,1280]{1,0:T(8,128)(2,1)} %get-tuple-element.99.z_ref.refs_0_), channel_id=1, source_target_pairs={{0,3},{1,0},{2,1},{3,2},{4,7},{5,4},{6,5},{7,6},{8,11},{9,8},{10,9... | collective-permute-start | bytes 2457608 | tf_op jit(solution)/shard_map/ppermute | solution.py:564
  197.4 23.8 %copy-start.26 = (bf16[320,1280]{1,0:T(8,128)(2,1)}, bf16[320,1280]{1,0:T(8,128)(2,1)S(1)}, u32[]{:S(2)}) copy-start(bf16[320,1280]{1,0:T(8,128)(2,1)S(1)} %collective-permute-done.9.gb_ref.refs_11_) | copy-start | bytes 2457604
  197.4 23.8 %collective-permute-start.13 = (bf16[160,1280]{1,0:T(8,128)(2,1)S(1)}, bf16[160,1280]{1,0:T(8,128)(2,1)S(1)}, u32[]{:S(2)}, u32[]{:S(2)}) collective-permute-start(bf16[160,1280]{1,0:T(8,128)(2,1)S(1)} %slice.296), channel_id=1, source_target_pairs={{0,1},{1,2},{2,3},{3,0},{4,5},{5,6},{6,7},{7,4},{8,9},{9,10},{10,1... | collective-permute-start | bytes 1228808 | tf_op jit(solution)/shard_map/ppermute | solution.py:560
  197.5 23.8 %copy-start.27 = (bf16[320,1280]{1,0:T(8,128)(2,1)}, bf16[320,1280]{1,0:T(8,128)(2,1)S(1)}, u32[]{:S(2)}) copy-start(bf16[320,1280]{1,0:T(8,128)(2,1)S(1)} %collective-permute-done.14.gb_ref.refs_9_) | copy-start | bytes 2457604
  197.6 27.0 %collective-permute-start.15 = (bf16[160,1280]{1,0:T(8,128)(2,1)S(1)}, bf16[160,1280]{1,0:T(8,128)(2,1)S(1)}, u32[]{:S(2)}, u32[]{:S(2)}) collective-permute-start(bf16[160,1280]{1,0:T(8,128)(2,1)S(1)} %slice.297), channel_id=1, source_target_pairs={{0,3},{1,0},{2,1},{3,2},{4,7},{5,4},{6,5},{7,6},{8,11},{9,8},{10,9... | collective-permute-start | bytes 1228808 | tf_op jit(solution)/shard_map/ppermute | solution.py:564
  215.0 10.6 %collective-permute-start.10 = (bf16[160,1280]{1,0:T(8,128)(2,1)S(1)}, bf16[160,1280]{1,0:T(8,128)(2,1)S(1)}, u32[]{:S(2)}, u32[]{:S(2)}) collective-permute-start(bf16[160,1280]{1,0:T(8,128)(2,1)S(1)} %slice.294), channel_id=1, source_target_pairs={{0,1},{1,2},{2,3},{3,0},{4,5},{5,6},{6,7},{7,4},{8,9},{9,10},{10,1... | collective-permute-start | bytes 1228808 | tf_op jit(solution)/shard_map/ppermute | solution.py:560
  221.3 8.8 %collective-permute-start.12 = (bf16[160,1280]{1,0:T(8,128)(2,1)S(1)}, bf16[160,1280]{1,0:T(8,128)(2,1)S(1)}, u32[]{:S(2)}, u32[]{:S(2)}) collective-permute-start(bf16[160,1280]{1,0:T(8,128)(2,1)S(1)} %slice.295), channel_id=1, source_target_pairs={{0,3},{1,0},{2,1},{3,2},{4,7},{5,4},{6,5},{7,6},{8,11},{9,8},{10,9... | collective-permute-start | bytes 1228808 | tf_op jit(solution)/shard_map/ppermute | solution.py:564
  243.3 27.1 %collective-permute-start.20 = (bf16[160,1280]{1,0:T(8,128)(2,1)S(1)}, bf16[160,1280]{1,0:T(8,128)(2,1)S(1)}, u32[]{:S(2)}, u32[]{:S(2)}) collective-permute-start(bf16[160,1280]{1,0:T(8,128)(2,1)S(1)} %get-tuple-element.225), channel_id=1, source_target_pairs={{0,3},{1,0},{2,1},{3,2},{4,7},{5,4},{6,5},{7,6},{8,11},{9,8},{10,9... | collective-permute-start | bytes 1228808 | tf_op jit(solution)/shard_map/ppermute | solution.py:564
  270.3 12.5 %collective-permute-start.22 = (bf16[160,1280]{1,0:T(8,128)(2,1)S(1)}, bf16[160,1280]{1,0:T(8,128)(2,1)S(1)}, u32[]{:S(2)}, u32[]{:S(2)}) collective-permute-start(bf16[160,1280]{1,0:T(8,128)(2,1)S(1)} %get-tuple-element.224), channel_id=1, source_target_pairs={{0,1},{1,2},{2,3},{3,0},{4,5},{5,6},{6,7},{7,4},{8,9},{9,10},{10,1... | collective-permute-start | bytes 1228808 | tf_op jit(solution)/shard_map/ppermute | solution.py:560
  270.6 24.5 %collective-permute-start.21 = (bf16[320,1280]{1,0:T(8,128)(2,1)S(1)}, bf16[320,1280]{1,0:T(8,128)(2,1)S(1)}, u32[]{:S(2)}, u32[]{:S(2)}) collective-permute-start(bf16[320,1280]{1,0:T(8,128)(2,1)S(1)} %pad_maximum_fusion.4), channel_id=1, source_target_pairs={{0,3},{1,0},{2,1},{3,2},{4,7},{5,4},{6,5},{7,6},{8,11},{9,8},{10,9... | collective-permute-start | bytes 2457608 | tf_op jit(solution)/shard_map/ppermute | solution.py:564
  283.0 14.4 %collective-permute-start.23 = (bf16[320,1280]{1,0:T(8,128)(2,1)S(1)}, bf16[320,1280]{1,0:T(8,128)(2,1)S(1)}, u32[]{:S(2)}, u32[]{:S(2)}) collective-permute-start(bf16[320,1280]{1,0:T(8,128)(2,1)S(1)} %pad_maximum_fusion.5), channel_id=1, source_target_pairs={{0,1},{1,2},{2,3},{3,0},{4,5},{5,6},{6,7},{7,4},{8,9},{9,10},{10,1... | collective-permute-start | bytes 2457608 | tf_op jit(solution)/shard_map/ppermute | solution.py:560
  303.9 18.1 %collective-permute-start.24 = (bf16[320,1280]{1,0:T(8,128)(2,1)}, bf16[320,1280]{1,0:T(8,128)(2,1)S(1)}, u32[]{:S(2)}, u32[]{:S(2)}) collective-permute-start(bf16[320,1280]{1,0:T(8,128)(2,1)} %get-tuple-element.112.x_ref.p0), channel_id=1, source_target_pairs={{0,1},{1,2},{2,3},{3,0},{4,5},{5,6},{6,7},{7,4},{8,9},{9,10},{10,1... | collective-permute-start | bytes 2457608 | tf_op jit(solution)/shard_map/ppermute | solution.py:560
  304.1 18.0 %collective-permute-start.26 = (bf16[320,1280]{1,0:T(8,128)(2,1)}, bf16[320,1280]{1,0:T(8,128)(2,1)S(1)}, u32[]{:S(2)}, u32[]{:S(2)}) collective-permute-start(bf16[320,1280]{1,0:T(8,128)(2,1)} %get-tuple-element.112.x_ref.p0), channel_id=1, source_target_pairs={{0,3},{1,0},{2,1},{3,2},{4,7},{5,4},{6,5},{7,6},{8,11},{9,8},{10,9... | collective-permute-start | bytes 2457608 | tf_op jit(solution)/shard_map/ppermute | solution.py:564
  322.0 13.5 %collective-permute-start.25 = (bf16[160,1280]{1,0:T(8,128)(2,1)S(1)}, bf16[160,1280]{1,0:T(8,128)(2,1)S(1)}, u32[]{:S(2)}, u32[]{:S(2)}) collective-permute-start(bf16[160,1280]{1,0:T(8,128)(2,1)S(1)} %slice.300), channel_id=1, source_target_pairs={{0,1},{1,2},{2,3},{3,0},{4,5},{5,6},{6,7},{7,4},{8,9},{9,10},{10,1... | collective-permute-start | bytes 1228808 | tf_op jit(solution)/shard_map/ppermute | solution.py:560
  322.1 13.4 %collective-permute-start.27 = (bf16[160,1280]{1,0:T(8,128)(2,1)S(1)}, bf16[160,1280]{1,0:T(8,128)(2,1)S(1)}, u32[]{:S(2)}, u32[]{:S(2)}) collective-permute-start(bf16[160,1280]{1,0:T(8,128)(2,1)S(1)} %slice.301), channel_id=1, source_target_pairs={{0,3},{1,0},{2,1},{3,2},{4,7},{5,4},{6,5},{7,6},{8,11},{9,8},{10,9... | collective-permute-start | bytes 1228808 | tf_op jit(solution)/shard_map/ppermute | solution.py:564
  377.0 166.5 %reduce-scatter.5.cloned.1.call-start = ((), (), s32[]{:S(2)}) async-start(), calls=%async_computation.11 | async-start | bytes 6963200 | tf_op jit(solution)/shard_map/reduce_scatter | solution.py:668
  397.8 11.6 %collective-permute-start.16 = (bf16[160,1280]{1,0:T(8,128)(2,1)S(1)}, bf16[160,1280]{1,0:T(8,128)(2,1)S(1)}, u32[]{:S(2)}, u32[]{:S(2)}) collective-permute-start(bf16[160,1280]{1,0:T(8,128)(2,1)S(1)} %get-tuple-element.227), channel_id=1, source_target_pairs={{0,3},{1,0},{2,1},{3,2},{4,7},{5,4},{6,5},{7,6},{8,11},{9,8},{10,9... | collective-permute-start | bytes 1228808 | tf_op jit(solution)/shard_map/ppermute | solution.py:564
  401.5 22.5 %collective-permute-start.18 = (bf16[160,1280]{1,0:T(8,128)(2,1)S(1)}, bf16[160,1280]{1,0:T(8,128)(2,1)S(1)}, u32[]{:S(2)}, u32[]{:S(2)}) collective-permute-start(bf16[160,1280]{1,0:T(8,128)(2,1)S(1)} %get-tuple-element.226), channel_id=1, source_target_pairs={{0,1},{1,2},{2,3},{3,0},{4,5},{5,6},{6,7},{7,4},{8,9},{9,10},{10,1... | collective-permute-start | bytes 1228808 | tf_op jit(solution)/shard_map/ppermute | solution.py:560
  409.5 44.5 %collective-permute-start.17 = (bf16[320,1280]{1,0:T(8,128)(2,1)S(1)}, bf16[320,1280]{1,0:T(8,128)(2,1)}, u32[]{:S(2)}, u32[]{:S(2)}) collective-permute-start(bf16[320,1280]{1,0:T(8,128)(2,1)S(1)} %pad_maximum_fusion.2), channel_id=1, source_target_pairs={{0,3},{1,0},{2,1},{3,2},{4,7},{5,4},{6,5},{7,6},{8,11},{9,8},{10,9... | collective-permute-start | bytes 2457608 | tf_op jit(solution)/shard_map/ppermute | solution.py:564
  422.8 12.3 %collective-permute-start.28 = (bf16[160,1280]{1,0:T(8,128)(2,1)S(1)}, bf16[160,1280]{1,0:T(8,128)(2,1)S(1)}, u32[]{:S(2)}, u32[]{:S(2)}) collective-permute-start(bf16[160,1280]{1,0:T(8,128)(2,1)S(1)} %get-tuple-element.223), channel_id=1, source_target_pairs={{0,3},{1,0},{2,1},{3,2},{4,7},{5,4},{6,5},{7,6},{8,11},{9,8},{10,9... | collective-permute-start | bytes 1228808 | tf_op jit(solution)/shard_map/ppermute | solution.py:564
  424.2 29.9 %collective-permute-start.19 = (bf16[320,1280]{1,0:T(8,128)(2,1)S(1)}, bf16[320,1280]{1,0:T(8,128)(2,1)S(1)}, u32[]{:S(2)}, u32[]{:S(2)}) collective-permute-start(bf16[320,1280]{1,0:T(8,128)(2,1)S(1)} %pad_maximum_fusion.3), channel_id=1, source_target_pairs={{0,1},{1,2},{2,3},{3,0},{4,5},{5,6},{6,7},{7,4},{8,9},{9,10},{10,1... | collective-permute-start | bytes 2457608 | tf_op jit(solution)/shard_map/ppermute | solution.py:560
  425.2 27.8 %collective-permute-start.30 = (bf16[160,1280]{1,0:T(8,128)(2,1)S(1)}, bf16[160,1280]{1,0:T(8,128)(2,1)S(1)}, u32[]{:S(2)}, u32[]{:S(2)}) collective-permute-start(bf16[160,1280]{1,0:T(8,128)(2,1)S(1)} %get-tuple-element.222), channel_id=1, source_target_pairs={{0,1},{1,2},{2,3},{3,0},{4,5},{5,6},{6,7},{7,4},{8,9},{9,10},{10,1... | collective-permute-start | bytes 1228808 | tf_op jit(solution)/shard_map/ppermute | solution.py:560
  435.3 31.8 %collective-permute-start.29 = (bf16[320,1280]{1,0:T(8,128)(2,1)S(1)}, bf16[320,1280]{1,0:T(8,128)(2,1)}, u32[]{:S(2)}, u32[]{:S(2)}) collective-permute-start(bf16[320,1280]{1,0:T(8,128)(2,1)S(1)} %pad_maximum_fusion.6), channel_id=1, source_target_pairs={{0,3},{1,0},{2,1},{3,2},{4,7},{5,4},{6,5},{7,6},{8,11},{9,8},{10,9... | collective-permute-start | bytes 2457608 | tf_op jit(solution)/shard_map/ppermute | solution.py:564
  453.1 14.0 %collective-permute-start.31 = (bf16[320,1280]{1,0:T(8,128)(2,1)S(1)}, bf16[320,1280]{1,0:T(8,128)(2,1)}, u32[]{:S(2)}, u32[]{:S(2)}) collective-permute-start(bf16[320,1280]{1,0:T(8,128)(2,1)S(1)} %pad_maximum_fusion.7), channel_id=1, source_target_pairs={{0,1},{1,2},{2,3},{3,0},{4,5},{5,6},{6,7},{7,4},{8,9},{9,10},{10,1... | collective-permute-start | bytes 2457608 | tf_op jit(solution)/shard_map/ppermute | solution.py:560
  459.7 20.7 %all-to-all-start.2 = ((bf16[4,320,320]{2,1,0:T(8,128)(2,1)}), bf16[4,320,320]{2,1,0:T(8,128)(2,1)S(1)}, u32[]{:S(2)}, u32[]{:S(2)}) async-start(bf16[4,320,320]{2,1,0:T(8,128)(2,1)} %result.1), calls=%async_computation.2 | async-start | bytes 1966080 | tf_op jit(solution)/shard_map/all_to_all | solution.py:693
  489.1 18.5 %all-to-all-start.3 = ((bf16[4,320,320]{2,1,0:T(8,128)(2,1)}), bf16[4,320,320]{2,1,0:T(8,128)(2,1)}, u32[]{:S(2)}, u32[]{:S(2)}) async-start(bf16[4,320,320]{2,1,0:T(8,128)(2,1)} %get-tuple-element.119), calls=%async_computation.3 | async-start | bytes 1966080 | tf_op jit(solution)/shard_map/all_to_all | solution.py:689
  507.6 26.6 %all-to-all-start.5 = ((bf16[32,2,6960]{2,1,0:T(2,128)(2,1)}), bf16[32,2,6960]{2,1,0:T(2,128)(2,1)}, u32[]{:S(2)}, u32[]{:S(2)}) async-start(bf16[32,2,6960]{2,1,0:T(2,128)(2,1)} %reshape.372), calls=%async_computation.5 | async-start | bytes 1802240 | tf_op jit(solution)/shard_map/all_to_all | solution.py:584
  542.0 9.7 %collective-permute-start.32 = (bf16[80,1280]{1,0:T(8,128)(2,1)}, bf16[80,1280]{1,0:T(8,128)(2,1)S(1)}, u32[]{:S(2)}, u32[]{:S(2)}) collective-permute-start(bf16[80,1280]{1,0:T(8,128)(2,1)} %reduce-scatter.3.cloned.1.call-done), channel_id=1, source_target_pairs={{0,4},{4,0},{1,5},{5,1},{2,6},{6,2},{3,7},{7,3},{8,12},{12,8},{9,1... | collective-permute-start | bytes 614408 | tf_op jit(solution)/shard_map/ppermute | solution.py:717
  543.5 15.7 %collective-permute-start.33 = (bf16[80,2560]{1,0:T(8,128)(2,1)}, bf16[80,2560]{1,0:T(8,128)(2,1)S(1)}, u32[]{:S(2)}, u32[]{:S(2)}) collective-permute-start(bf16[80,2560]{1,0:T(8,128)(2,1)} %reduce-scatter.5.cloned.1.call-done), channel_id=1, source_target_pairs={{0,4},{4,0},{1,5},{5,1},{2,6},{6,2},{3,7},{7,3},{8,12},{12,8},{9,1... | collective-permute-start | bytes 1228808 | tf_op jit(solution)/shard_map/ppermute | solution.py:716
  (49 other events, 456.8 us)
Sparse Core Ops, SparseCore 0:
  10.3 38.3 all-gather.2
  50.9 43.5 all-gather.4
  377.1 68.2 reduce-scatter.2
  447.6 82.9 reduce-scatter.4
